TPU v7x, 512 devices: a whole 4x8x8 slice. The times are simulated.
512 devices in a mesh: ctx: 16 (over x_lo, z), ch: 32 (over x_hi, y, core).
Axes of the slice: x: 4 (x_hi: 2, x_lo: 2; x = x_hi * 2 + x_lo), y: 8, z: 8, core: 2. Of those that a mesh axis runs over, the one named last changes fastest.
Arguments:
- tokens: bfloat16 [2048, 4096], P('ctx', 'ch'), may hold values from -6 to 6
- in_weight: bfloat16 [4096, 3, 4096], P(None, None, 'ch'), may hold values from -0.09375 to 0.09375
- filter_taps: float32 [2048, 4096], P('ctx', 'ch'), may hold values from -0.125 to 0.125
- grad_out: bfloat16 [2048, 4096], P('ctx', 'ch'), may hold values from -0.125 to 0.125
Outputs:
- weight_grad: float32 [4096, 3, 4096], P('ctx', None, 'ch')
- filter_grad: float32 [2048, 4096], P('ctx', 'ch')
All inputs are finite; a program needn't handle non-finite values.
Results may differ from a plain program's by a relative error of at most 0.029.
Values may be sent and summed in bfloat16 or wider, within the bound.
A program may use at most 64 MiB of HBM per device.

v0:
```python
import math

import jax
import jax.numpy as jnp
from jax import lax
from jax.sharding import PartitionSpec as P


def swapped(block, axis, apart):
    count = lax.axis_size(axis)
    route = []
    for low in range(count):
        high = low | 1 << apart
        if high != low and high < count:
            route += [(low, high), (high, low)]
    return lax.ppermute(block, axis, route)


def unit_roots(numerator, denominator):
    reduced = jnp.mod(numerator, denominator).astype(jnp.float32)
    angles = reduced * (-2.0 * math.pi / denominator)
    return jnp.stack([jnp.cos(angles), jnp.sin(angles)])


def complex_product(left, right):
    return jnp.stack(
        [left[0] * right[0] - left[1] * right[1], left[0] * right[1] + left[1] * right[0]]
    )


def complex_einsum(pattern, dft_table, values):
    highest = lax.Precision.HIGHEST
    real_part = jnp.einsum(pattern, dft_table[0], values[0], precision=highest) - jnp.einsum(
        pattern, dft_table[1], values[1], precision=highest
    )
    imag_part = jnp.einsum(pattern, dft_table[0], values[1], precision=highest) + jnp.einsum(
        pattern, dft_table[1], values[0], precision=highest
    )
    return jnp.stack([real_part, imag_part])


def local_transform(values, direction):
    length = values.shape[1]
    local_index = jnp.arange(length)
    dft_table = unit_roots(direction * local_index[:, None] * local_index[None, :], length)
    return complex_einsum("km,mfn->kfn", dft_table, values)


def bit_reverse(device, steps_count):
    flipped = jnp.zeros((), jnp.int32)
    for bit_index in range(steps_count):
        flipped = flipped + ((device >> bit_index & 1) << steps_count - 1 - bit_index)
    return flipped


def butterfly_section(values, bit_index, device, direction):
    partner = swapped(values.astype(jnp.bfloat16), "ctx", bit_index).astype(values.dtype)
    half_span = 1 << bit_index
    is_upper = device >> bit_index & 1 == 1
    root_value = unit_roots(direction * (device % half_span), 2 * half_span).reshape(2, 1, 1, 1)
    if direction > 0:
        lower_value = values + partner
        upper_value = complex_product(partner - values, root_value)
    else:
        lower_value = values + complex_product(partner, root_value)
        upper_value = partner - complex_product(values, root_value)
    return jnp.where(is_upper, upper_value, lower_value)


def cross_forward(values, total_len):
    device = lax.axis_index("ctx")
    ctx_count = lax.axis_size("ctx")
    length = values.shape[1]
    steps_count = ctx_count.bit_length() - 1
    for bit_index in reversed(range(steps_count)):
        values = butterfly_section(values, bit_index, device, 1)
    reversed_index = bit_reverse(device, steps_count)
    twist_table = unit_roots(jnp.arange(length) * reversed_index, total_len)
    values = complex_product(values, twist_table[:, :, None, None])
    return local_transform(values, 1)


def cross_inverse(values, total_len):
    device = lax.axis_index("ctx")
    ctx_count = lax.axis_size("ctx")
    length = values.shape[1]
    values = local_transform(values, -1)
    steps_count = ctx_count.bit_length() - 1
    reversed_index = bit_reverse(device, steps_count)
    twist_table = unit_roots(-(jnp.arange(length) * reversed_index), total_len)
    values = complex_product(values, twist_table[:, :, None, None])
    for bit_index in range(steps_count):
        values = butterfly_section(values, bit_index, device, -1)
    return values


def spectra_mix(filter_spec, product_spec, grad_spec):
    filter_conj = jnp.stack([filter_spec[0], -filter_spec[1]])
    product_conj = jnp.stack([product_spec[0], -product_spec[1]])
    return jnp.stack(
        [
            complex_product(filter_spec, product_spec),
            complex_product(filter_conj, grad_spec),
            complex_product(grad_spec, product_conj),
        ],
        axis=2,
    )


def on_device(tokens, in_weight, filter_taps, grad_out):
    tok_rows = tokens.shape[0]
    channels = filter_taps.shape[1]
    ctx_count = lax.axis_size("ctx")
    total_len = tok_rows * ctx_count
    device = lax.axis_index("ctx")
    features = lax.all_gather(tokens, "ch", axis=1, tiled=True)
    projected = jnp.einsum(
        "nd,djc->njc", features, in_weight, preferred_element_type=jnp.float32
    ).astype(jnp.bfloat16)
    query_proj = projected[:, 0].astype(jnp.float32)
    key_proj = projected[:, 1].astype(jnp.float32)
    value_proj = projected[:, 2].astype(jnp.float32)
    upstream = grad_out.astype(jnp.float32)
    product = key_proj * value_proj
    grad_z = upstream * query_proj
    fields = jnp.stack([filter_taps, product, grad_z], axis=1)
    positions = device * tok_rows + jnp.arange(tok_rows)
    shift_table = unit_roots(positions, 2 * total_len)
    plain = jnp.stack([fields, jnp.zeros_like(fields)])
    twisted = shift_table[:, :, None, None] * fields[None]
    values = jnp.concatenate([plain, twisted], axis=2)
    spectra = cross_forward(values, total_len).reshape(2, tok_rows, 2, 3, channels)
    mixed = jnp.stack(
        [
            spectra_mix(spectra[:, :, half, 0], spectra[:, :, half, 1], spectra[:, :, half, 2])
            for half in range(2)
        ],
        axis=2,
    )
    restored = cross_inverse(mixed.reshape(2, tok_rows, 6, channels), total_len).reshape(
        2, tok_rows, 2, 3, channels
    )
    time_fields = (
        restored[0, :, 0]
        + shift_table[0][:, None, None] * restored[0, :, 1]
        + shift_table[1][:, None, None] * restored[1, :, 1]
    )
    time_fields = time_fields * (1.0 / (2 * total_len))
    conv_out = time_fields[:, 0]
    grad_mix = time_fields[:, 1]
    filter_grad = time_fields[:, 2]
    grad_query = (upstream * conv_out).astype(jnp.bfloat16)
    grad_key = (grad_mix * value_proj).astype(jnp.bfloat16)
    grad_value = (grad_mix * key_proj).astype(jnp.bfloat16)
    grad_proj = jnp.stack([grad_query, grad_key, grad_value], axis=1)
    weight_grad = lax.psum_scatter(
        jnp.einsum("nd,njc->djc", features, grad_proj, preferred_element_type=jnp.float32).astype(
            jnp.bfloat16
        ),
        "ctx",
        scatter_dimension=0,
        tiled=True,
    ).astype(jnp.float32)
    return (weight_grad, filter_grad)


def solution(mesh):
    placed = (P("ctx", "ch"), P(None, None, "ch"), P("ctx", "ch"), P("ctx", "ch"))
    return jax.shard_map(
        on_device,
        mesh=mesh,
        in_specs=placed,
        out_specs=(P("ctx", None, "ch"), P("ctx", "ch")),
        check_vma=False,
    )
```

profile of v0, /device:TPU:24, one launch (start us, length us, event | category | flops | bytes accessed | tf_op | source)
XLA Modules:
  0.0 348.3 jit_solution(8341127453749219551)
XLA Ops:
  8.1 83.9 %all-gather.2.cloned.1.call-done = bf16[128,4096]{1,0:T(8,128)(2,1)} async-done(((bf16[128,128]{1,0:T(8,128)(2,1)}), bf16[128,4096]{1,0:T(8,128)(2,1)}) %all-gather.2.cloned.1.call-update) | async-done | bytes 1048592 | tf_op jit(solution)/shard_map/all_gather | solution.py:116
  91.9 1.9 convolution_convert_fusion.1
  95.4 2.5 collective-permute-start
  98.1 10.8 %collective-permute-done = bf16[2,128,6,128]{3,1,2,0:T(8,128)(2,1)} collective-permute-done((bf16[2,128,6,128]{3,1,2,0:T(8,128)(2,1)}, bf16[2,128,6,128]{3,1,2,0:T(8,128)(2,1)}, u32[]{:S(2)}, u32[]{:S(2)}) %collective-permute-start) | collective-permute-done | bytes 393248 | tf_op jit(solution)/shard_map/ppermute | solution.py:16
  110.1 2.2 fusion.129
  112.3 8.0 %collective-permute-start.1 = (bf16[2,128,6,128]{3,1,2,0:T(8,128)(2,1)}, bf16[2,128,6,128]{3,1,2,0:T(8,128)(2,1)S(1)}, u32[]{:S(2)}, u32[]{:S(2)}) collective-permute-start(bf16[2,128,6,128]{3,1,2,0:T(8,128)(2,1)} %get-tuple-element.17), channel_id=1, source_target_pairs={{0,128},{128,0},{32,160},{160,32},{64,192},{192,64},{96,224},{224,... | collective-permute-start | bytes 1179656 | tf_op jit(solution)/shard_map/ppermute | solution.py:16
  120.5 12.1 %collective-permute-done.1 = bf16[2,128,6,128]{3,1,2,0:T(8,128)(2,1)S(1)} collective-permute-done((bf16[2,128,6,128]{3,1,2,0:T(8,128)(2,1)}, bf16[2,128,6,128]{3,1,2,0:T(8,128)(2,1)S(1)}, u32[]{:S(2)}, u32[]{:S(2)}) %collective-permute-start.1) | collective-permute-done | bytes 393248 | tf_op jit(solution)/shard_map/ppermute | solution.py:16
  132.6 1.2 convert_subtract_fusion.2
  133.9 1.2 fusion.127
  135.1 9.4 %collective-permute-start.2 = (bf16[2,128,6,128]{3,1,2,0:T(8,128)(2,1)}, bf16[2,128,6,128]{3,1,2,0:T(8,128)(2,1)S(1)}, u32[]{:S(2)}, u32[]{:S(2)}) collective-permute-start(bf16[2,128,6,128]{3,1,2,0:T(8,128)(2,1)} %get-tuple-element.15), channel_id=1, source_target_pairs={{0,64},{64,0},{32,96},{96,32},{128,192},{192,128},{160,224},{224,1... | collective-permute-start | bytes 1179656 | tf_op jit(solution)/shard_map/ppermute | solution.py:16
  144.7 14.5 %collective-permute-done.2 = bf16[2,128,6,128]{3,1,2,0:T(8,128)(2,1)S(1)} collective-permute-done((bf16[2,128,6,128]{3,1,2,0:T(8,128)(2,1)}, bf16[2,128,6,128]{3,1,2,0:T(8,128)(2,1)S(1)}, u32[]{:S(2)}, u32[]{:S(2)}) %collective-permute-start.2) | collective-permute-done | bytes 393248 | tf_op jit(solution)/shard_map/ppermute | solution.py:16
  159.2 1.2 convert_subtract_fusion.1
  161.7 1.9 collective-permute-start.3
  163.7 11.1 %collective-permute-done.3 = bf16[2,128,6,128]{3,1,2,0:T(8,128)(2,1)S(1)} collective-permute-done((bf16[2,128,6,128]{3,1,2,0:T(8,128)(2,1)}, bf16[2,128,6,128]{3,1,2,0:T(8,128)(2,1)S(1)}, u32[]{:S(2)}, u32[]{:S(2)}) %collective-permute-start.3) | collective-permute-done | bytes 393248 | tf_op jit(solution)/shard_map/ppermute | solution.py:16
  174.8 1.2 convert_subtract_fusion
  183.2 2.2 collective-permute-start.4
  185.5 9.8 %collective-permute-done.4 = bf16[2,128,6,128]{3,1,2,0:T(8,128)(2,1)S(1)} collective-permute-done((bf16[2,128,6,128]{3,1,2,0:T(8,128)(2,1)S(1)}, bf16[2,128,6,128]{3,1,2,0:T(8,128)(2,1)S(1)}, u32[]{:S(2)}, u32[]{:S(2)}) %collective-permute-start.4) | collective-permute-done | bytes 393248 | tf_op jit(solution)/shard_map/ppermute | solution.py:16
  195.5 1.2 fusion.123
  196.7 1.9 collective-permute-start.5
  198.8 1.3 multiply_subtract_fusion.5
  200.1 17.3 %collective-permute-done.5 = bf16[2,128,6,128]{3,1,2,0:T(8,128)(2,1)S(1)} collective-permute-done((bf16[2,128,6,128]{3,1,2,0:T(8,128)(2,1)}, bf16[2,128,6,128]{3,1,2,0:T(8,128)(2,1)S(1)}, u32[]{:S(2)}, u32[]{:S(2)}) %collective-permute-start.5) | collective-permute-done | bytes 393248 | tf_op jit(solution)/shard_map/ppermute | solution.py:16
  217.6 1.2 fusion.121
  218.8 8.0 %collective-permute-start.6 = (bf16[2,128,6,128]{3,1,2,0:T(8,128)(2,1)}, bf16[2,128,6,128]{3,1,2,0:T(8,128)(2,1)S(1)}, u32[]{:S(2)}, u32[]{:S(2)}) collective-permute-start(bf16[2,128,6,128]{3,1,2,0:T(8,128)(2,1)} %get-tuple-element.6), channel_id=1, source_target_pairs={{0,128},{128,0},{32,160},{160,32},{64,192},{192,64},{96,224},{224,... | collective-permute-start | bytes 1179656 | tf_op jit(solution)/shard_map/ppermute | solution.py:16
  227.0 1.3 multiply_subtract_fusion.3
  228.3 15.9 %collective-permute-done.6 = bf16[2,128,6,128]{3,1,2,0:T(8,128)(2,1)S(1)} collective-permute-done((bf16[2,128,6,128]{3,1,2,0:T(8,128)(2,1)}, bf16[2,128,6,128]{3,1,2,0:T(8,128)(2,1)S(1)}, u32[]{:S(2)}, u32[]{:S(2)}) %collective-permute-start.6) | collective-permute-done | bytes 393248 | tf_op jit(solution)/shard_map/ppermute | solution.py:16
  244.4 1.2 fusion.119
  245.7 2.5 collective-permute-start.7
  248.4 1.3 multiply_subtract_fusion.1
  249.7 5.8 %collective-permute-done.7 = bf16[2,128,6,128]{3,1,2,0:T(8,128)(2,1)S(1)} collective-permute-done((bf16[2,128,6,128]{3,1,2,0:T(8,128)(2,1)}, bf16[2,128,6,128]{3,1,2,0:T(8,128)(2,1)S(1)}, u32[]{:S(2)}, u32[]{:S(2)}) %collective-permute-start.7) | collective-permute-done | bytes 393248 | tf_op jit(solution)/shard_map/ppermute | solution.py:16
  257.2 2.6 fusion
  259.9 79.8 %reduce-scatter.2.cloned.1.call-done = bf16[256,3,128]{0,2,1:T(8,128)(2,1)} async-done(((bf16[4096,3,128]{0,2,1:T(8,128)(2,1)}), bf16[256,3,128]{0,2,1:T(8,128)(2,1)}) %reduce-scatter.2.cloned.1.call-update) | async-done | bytes 196624 | tf_op jit(solution)/shard_map/reduce_scatter | solution.py:156
  339.6 1.8 copy.7
  (86 shorter events, 14.2 us)
Async XLA Ops:
  7.2 84.8 %copy-start = (bf16[4096,3,128]{2,0,1:T(8,128)(2,1)S(1)}, bf16[4096,3,128]{2,0,1:T(8,128)(2,1)}, u32[]{:S(2)}) copy-start(bf16[4096,3,128]{2,0,1:T(8,128)(2,1)} %param.5) | copy-start | bytes 9437188
  7.2 86.7 %copy-start.12 = (bf16[128,128]{1,0:T(8,128)(2,1)S(1)}, bf16[128,128]{1,0:T(8,128)(2,1)}, u32[]{:S(2)}) copy-start(bf16[128,128]{1,0:T(8,128)(2,1)} %param.7) | copy-start | bytes 98308
  7.2 86.7 %copy-start.14 = (f32[128,128]{1,0:T(8,128)S(1)}, f32[128,128]{1,0:T(8,128)}, u32[]{:S(2)}) copy-start(f32[128,128]{1,0:T(8,128)} %param.6) | copy-start | bytes 196612
  7.2 84.7 %all-gather.2.cloned.1.call-start = ((), (), s32[]{:S(2)}) async-start(), calls=%async_computation.1 | async-start | bytes 1081344 | tf_op jit(solution)/shard_map/all_gather | solution.py:116
  7.9 331.7 %reduce-scatter.2.cloned.1.call-start = ((), (), s32[]{:S(2)}) async-start(), calls=%async_computation.2 | async-start | bytes 3342336 | tf_op jit(solution)/shard_map/reduce_scatter | solution.py:156
  93.9 1.6 copy-start.10
  94.0 0.7 copy-start.8
  95.4 13.5 %collective-permute-start = (bf16[2,128,6,128]{3,1,2,0:T(8,128)(2,1)}, bf16[2,128,6,128]{3,1,2,0:T(8,128)(2,1)}, u32[]{:S(2)}, u32[]{:S(2)}) collective-permute-start(bf16[2,128,6,128]{3,1,2,0:T(8,128)(2,1)} %fusion.12), channel_id=1, source_target_pairs={{0,256},{256,0},{32,288},{288,32},{64,320},{320,64},{96,352},{352,... | collective-permute-start | bytes 1179656 | tf_op jit(solution)/shard_map/ppermute | solution.py:16
  98.1 12.0 %copy-start.9 = (f32[1,128,3,128]{3,1,2,0:T(8,128)S(1)}, f32[1,128,3,128]{3,1,2,0:T(8,128)}, u32[]{:S(2)}) copy-start(f32[1,128,3,128]{3,1,2,0:T(8,128)} %copy-done.8) | copy-start | bytes 589828
  112.3 20.3 %collective-permute-start.1 = (bf16[2,128,6,128]{3,1,2,0:T(8,128)(2,1)}, bf16[2,128,6,128]{3,1,2,0:T(8,128)(2,1)S(1)}, u32[]{:S(2)}, u32[]{:S(2)}) collective-permute-start(bf16[2,128,6,128]{3,1,2,0:T(8,128)(2,1)} %get-tuple-element.17), channel_id=1, source_target_pairs={{0,128},{128,0},{32,160},{160,32},{64,192},{192,64},{96,224},{224,... | collective-permute-start | bytes 1179656 | tf_op jit(solution)/shard_map/ppermute | solution.py:16
  120.5 13.4 %copy-start.3 = (f32[2,128,6,128]{3,1,2,0:T(8,128)S(1)}, f32[2,128,6,128]{3,1,2,0:T(8,128)}, u32[]{:S(2)}) copy-start(f32[2,128,6,128]{3,1,2,0:T(8,128)} %get-tuple-element.18) | copy-start | bytes 2359300
  135.1 24.1 %collective-permute-start.2 = (bf16[2,128,6,128]{3,1,2,0:T(8,128)(2,1)}, bf16[2,128,6,128]{3,1,2,0:T(8,128)(2,1)S(1)}, u32[]{:S(2)}, u32[]{:S(2)}) collective-permute-start(bf16[2,128,6,128]{3,1,2,0:T(8,128)(2,1)} %get-tuple-element.15), channel_id=1, source_target_pairs={{0,64},{64,0},{32,96},{96,32},{128,192},{192,128},{160,224},{224,1... | collective-permute-start | bytes 1179656 | tf_op jit(solution)/shard_map/ppermute | solution.py:16
  144.7 15.8 %copy-start.6 = (f32[2,128,6,128]{3,1,2,0:T(8,128)S(1)}, f32[2,128,6,128]{3,1,2,0:T(8,128)}, u32[]{:S(2)}) copy-start(f32[2,128,6,128]{3,1,2,0:T(8,128)} %get-tuple-element.16) | copy-start | bytes 2359300
  161.7 13.1 %collective-permute-start.3 = (bf16[2,128,6,128]{3,1,2,0:T(8,128)(2,1)}, bf16[2,128,6,128]{3,1,2,0:T(8,128)(2,1)S(1)}, u32[]{:S(2)}, u32[]{:S(2)}) collective-permute-start(bf16[2,128,6,128]{3,1,2,0:T(8,128)(2,1)} %get-tuple-element.13), channel_id=1, source_target_pairs={{0,32},{32,0},{64,96},{96,64},{128,160},{160,128},{192,224},{224,1... | collective-permute-start | bytes 1179656 | tf_op jit(solution)/shard_map/ppermute | solution.py:16
  163.6 12.5 %copy-start.5 = (f32[2,128,6,128]{3,1,2,0:T(8,128)S(1)}, f32[2,128,6,128]{3,1,2,0:T(8,128)}, u32[]{:S(2)}) copy-start(f32[2,128,6,128]{3,1,2,0:T(8,128)} %get-tuple-element.14) | copy-start | bytes 2359300
  183.2 12.1 %collective-permute-start.4 = (bf16[2,128,6,128]{3,1,2,0:T(8,128)(2,1)S(1)}, bf16[2,128,6,128]{3,1,2,0:T(8,128)(2,1)S(1)}, u32[]{:S(2)}, u32[]{:S(2)}) collective-permute-start(bf16[2,128,6,128]{3,1,2,0:T(8,128)(2,1)S(1)} %fusion.11), channel_id=1, source_target_pairs={{0,32},{32,0},{64,96},{96,64},{128,160},{160,128},{192,224},{224,1... | collective-permute-start | bytes 1179656 | tf_op jit(solution)/shard_map/ppermute | solution.py:16
  196.7 20.7 %collective-permute-start.5 = (bf16[2,128,6,128]{3,1,2,0:T(8,128)(2,1)}, bf16[2,128,6,128]{3,1,2,0:T(8,128)(2,1)S(1)}, u32[]{:S(2)}, u32[]{:S(2)}) collective-permute-start(bf16[2,128,6,128]{3,1,2,0:T(8,128)(2,1)} %get-tuple-element.8), channel_id=1, source_target_pairs={{0,64},{64,0},{32,96},{96,32},{128,192},{192,128},{160,224},{224,1... | collective-permute-start | bytes 1179656 | tf_op jit(solution)/shard_map/ppermute | solution.py:16
  198.8 18.8 %copy-start.1 = (f32[2,128,6,128]{3,1,2,0:T(8,128)S(1)}, f32[2,128,6,128]{3,1,2,0:T(8,128)}, u32[]{:S(2)}) copy-start(f32[2,128,6,128]{3,1,2,0:T(8,128)} %get-tuple-element.9) | copy-start | bytes 2359300
  218.8 25.4 %collective-permute-start.6 = (bf16[2,128,6,128]{3,1,2,0:T(8,128)(2,1)}, bf16[2,128,6,128]{3,1,2,0:T(8,128)(2,1)S(1)}, u32[]{:S(2)}, u32[]{:S(2)}) collective-permute-start(bf16[2,128,6,128]{3,1,2,0:T(8,128)(2,1)} %get-tuple-element.6), channel_id=1, source_target_pairs={{0,128},{128,0},{32,160},{160,32},{64,192},{192,64},{96,224},{224,... | collective-permute-start | bytes 1179656 | tf_op jit(solution)/shard_map/ppermute | solution.py:16
  227.0 17.4 %copy-start.2 = (f32[2,128,6,128]{3,1,2,0:T(8,128)S(1)}, f32[2,128,6,128]{3,1,2,0:T(8,128)}, u32[]{:S(2)}) copy-start(f32[2,128,6,128]{3,1,2,0:T(8,128)} %get-tuple-element.7) | copy-start | bytes 2359300
  245.7 9.9 %collective-permute-start.7 = (bf16[2,128,6,128]{3,1,2,0:T(8,128)(2,1)}, bf16[2,128,6,128]{3,1,2,0:T(8,128)(2,1)S(1)}, u32[]{:S(2)}, u32[]{:S(2)}) collective-permute-start(bf16[2,128,6,128]{3,1,2,0:T(8,128)(2,1)} %get-tuple-element.4), channel_id=1, source_target_pairs={{0,256},{256,0},{32,288},{288,32},{64,320},{320,64},{96,352},{352,... | collective-permute-start | bytes 1179656 | tf_op jit(solution)/shard_map/ppermute | solution.py:16
  248.4 7.4 %copy-start.4 = (f32[2,128,6,128]{3,1,2,0:T(8,128)S(1)}, f32[2,128,6,128]{3,1,2,0:T(8,128)}, u32[]{:S(2)}) copy-start(f32[2,128,6,128]{3,1,2,0:T(8,128)} %get-tuple-element.5) | copy-start | bytes 2359300
  255.6 0.9 copy-start.11
  255.6 1.5 copy-start.13
  255.6 1.5 copy-start.7
Sparse Core Ops, SparseCore 0:
  11.2 80.6 all-gather.1
  260.0 79.5 reduce-scatter.1
where the time goes:
time: 349 us; the launch traced here: 348 us
  waiting for transfers between devices  262 us (75%)
  starting transfers between devices  36.5 us (10%)
  other arithmetic  20.4 us (6%)
  between operations  15.8 us (5%)
  matrix products  11.1 us (3%)
    ppermute x8, waiting for transfers between devices, swapped(): return lax.ppermute(block, axis, route)  97.4 us
    all_gather x1, waiting for transfers between devices, on_device(): features = lax.all_gather(tokens, 'ch', axis=1, tiled=True)  83.9 us
    reduce_scatter x1, waiting for transfers between devices, on_device(): lax.psum_scatter(jnp.einsum('nd,njc->djc', features, grad_proj, preferred...  79.8 us
    ppermute x8, starting transfers between devices, swapped(): return lax.ppermute(block, axis, route)  36.4 us
    convert_element_type x8, other arithmetic, butterfly_section(): values.astype(jnp.bfloat16)  9.04 us
  transfers between devices with their start and end apart: 10, of which 10 were waited for; matrix products, arithmetic and copies ran while one was open for 1% of the time, Pallas kernels for 0%

commit v1 on v0

v1 whole, which is shorter than its diff:
```python
import math

import jax
import jax.numpy as jnp
import ml_dtypes
import numpy as np
from jax import lax
from jax.experimental import pallas as pl
from jax.experimental.pallas import tpu as pltpu
from jax.sharding import PartitionSpec as P

MESH = pl.DeviceIdType.MESH
BF16 = jnp.bfloat16
F32 = jnp.float32
ROWS = 128
TILES = 16
CHUNKS = 4


def transform_tables():
    r = np.arange(128)
    k1 = np.arange(128)
    forward = np.zeros((16, 256, 256))
    inverse = np.zeros((16, 256, 256))
    for k2 in range(1, 16):
        angle = 2 * np.pi * (((k2 + 32 * k1)[:, None] * r[None, :]) % 4096) / 4096
        c, s = np.cos(angle), np.sin(angle)
        forward[k2] = np.block([[c, s], [-s, c]])
        inverse[k2] = np.block([[c.T, -s.T], [s.T, c.T]]) * (2 / 4096)
    k1 = np.arange(64)
    a0 = 2 * np.pi * ((32 * k1[:, None] * r[None, :]) % 4096) / 4096
    a16 = 2 * np.pi * (((16 + 32 * k1)[:, None] * r[None, :]) % 4096) / 4096
    nyquist = 1.0 - 2.0 * (r % 2)
    re0, im0 = np.cos(a0), -np.sin(a0)
    im0[0] = nyquist
    zero = np.zeros((64, 128))
    forward[0] = np.block(
        [
            [re0, zero],
            [zero, np.cos(a16)],
            [im0, zero],
            [zero, -np.sin(a16)],
        ]
    )
    back_re0, back_im0 = 2 * np.cos(a0).T, -2 * np.sin(a0).T
    back_re0[:, 0] = 1.0
    back_im0[:, 0] = nyquist
    zero = np.zeros((128, 64))
    inverse[0] = (
        np.block(
            [
                [back_re0, zero, back_im0, zero],
                [zero, 2 * np.cos(a16).T, zero, -2 * np.sin(a16).T],
            ]
        )
        / 4096
    )
    block = np.arange(16)[:, None]
    k = np.arange(16)[None, :]
    angle = 2 * np.pi * ((block * k) % 32) / 32
    im_part = -np.sin(angle)
    im_part[:, 0] = 1.0 - 2.0 * (np.arange(16) % 2)
    single = np.concatenate([np.cos(angle), im_part], axis=1)
    single = np.broadcast_to(single[:, :, None], (16, 32, 128))
    return (
        forward.astype(ml_dtypes.bfloat16),
        inverse.astype(ml_dtypes.bfloat16),
        single.astype(np.float32),
    )


def root(n, a, sign):
    angle = -sign * 2 * math.pi * a / n
    return math.cos(angle), math.sin(angle)


def times(v, w):
    re, im = v
    wr, wi = w
    if abs(wi) < 1e-12:
        return (re, im) if wr > 0 else (-re, -im)
    if abs(wr) < 1e-12:
        return (-im, re) if wi > 0 else (im, -re)
    return re * wr - im * wi, re * wi + im * wr


def complex_dft(u, sign):
    n = len(u)
    if n == 1:
        return u
    h = n // 2
    low = [(u[a][0] + u[a + h][0], u[a][1] + u[a + h][1]) for a in range(h)]
    high = [
        times((u[a][0] - u[a + h][0], u[a][1] - u[a + h][1]), root(n, a, sign))
        for a in range(h)
    ]
    even, odd = complex_dft(low, sign), complex_dft(high, sign)
    return [even[i // 2] if i % 2 == 0 else odd[i // 2] for i in range(n)]


def real_forward(n, x):
    if n == 2:
        return [(x[0] + x[1], None), (x[0] - x[1], None)]
    h, q = n // 2, n // 4
    if len(x) == h:
        fold, diff = x, x
    else:
        fold = [x[a] + x[a + h] for a in range(h)]
        diff = [x[a] - x[a + h] for a in range(h)]
    even = real_forward(h, fold)
    odd = complex_dft(
        [times((diff[a], -diff[a + q]), root(n, a, 1)) for a in range(q)], 1
    )
    out = [None] * (h + 1)
    for m in range(h // 2 + 1):
        out[2 * m] = even[m]
    for j in range(q):
        k = 4 * j + 1
        if k <= h:
            out[k] = odd[j]
        else:
            out[n - k] = (odd[j][0], -odd[j][1])
    return out


def real_inverse(n, z, half=False):
    if n == 2:
        return [z[0][0] + z[1][0], z[0][0] - z[1][0]]
    h, q = n // 2, n // 4
    even = real_inverse(h, z[0::2])
    v = []
    for j in range(q):
        k = 4 * j + 1
        v.append(z[k] if k <= h else (z[n - k][0], -z[n - k][1]))
    s = complex_dft(v, -1)
    t = [times(s[a], root(n, a, -1)) for a in range(q)]
    odd = [t[a][0] for a in range(q)] + [-t[a][1] for a in range(q)]
    low = [even[a] + odd[a] for a in range(h)]
    return low if half else low + [even[a] - odd[a] for a in range(h)]


class Ring:
    def __init__(self, slot, half, place, right, left, send_sem, recv_sem):
        self.slot, self.half, self.place = slot, half, place
        self.to = (right, left)
        self.send_sem, self.recv_sem = send_sem, recv_sem

    def at(self, away):
        return lax.rem(self.place + 8 + away, 8)

    def copy(self, ref, way, step):
        return pltpu.make_async_remote_copy(
            src_ref=ref,
            dst_ref=ref,
            send_sem=self.send_sem.at[way, step - 1],
            recv_sem=self.recv_sem.at[way, step - 1],
            device_id=self.to[way],
            device_id_type=MESH,
        )

    def sent(self, way, step):
        away = (1 - step) if way == 0 else (step - 1)
        ref = self.slot(self.at(away))
        return self.copy(self.half(ref, way) if step == 4 else ref, way, step)

    def send(self, step):
        for way in range(2):
            self.sent(way, step).start()

    def wait(self, step):
        for way in range(2):
            ref = self.slot(self.at(-step if way == 0 else step))
            self.copy(self.half(ref, way) if step == 4 else ref, way, step).wait_recv()

    def drain(self):
        for step in range(1, 5):
            for way in range(2):
                self.sent(way, step).wait_send()


def half_of(rows):
    def half(ref, way):
        return ref.at[pl.ds(way * (rows // 2), rows // 2)]

    return half


def kernel(
    tok_ref, go_ref, taps_ref, w_hbm, f_hbm, g_hbm, ct_hbm,
    wg_ref, fg_ref,
    w_v, f_v, g_v, ct_v, tokb, gtb, gtx, qvb, qvx, tb, acc, bv, yb, fs, zb, gp,
    rown, rsend, rrecv, fown, fsend, frecv,
    local_sem, ra_s, ra_r, rb_s, rb_r, ga_s, ga_r, gb_s, gb_r, qa_s, qa_r, qb_s, qb_r,
    pair_s, pair_r, sib_s, sib_r, tr_s, tr_r, ty_s, ty_r, tx_s, tx_r, tx2_s, tx2_r, ts_s, ts_r,
):
    ctx, ch = lax.axis_index("ctx"), lax.axis_index("ch")
    xl, z = ctx // 8, lax.rem(ctx, 8)
    c, xh, y = lax.rem(ch, 2), ch // 16, lax.rem(ch // 2, 8)
    ox, oh, oc = 1 - xl, 1 - xh, 1 - c

    def dev(xh_, xl_, y_, z_, c_):
        return (xl_ * 8 + z_, (xh_ * 8 + y_) * 2 + c_)

    def remote(src, dst, s, r, to):
        return pltpu.make_async_remote_copy(
            src_ref=src, dst_ref=dst, send_sem=s, recv_sem=r, device_id=to, device_id_type=MESH
        )

    def turn(v, by):
        return lax.rem(v + 8 + by, 8)

    loads = [
        pltpu.make_async_copy(w_hbm, w_v, local_sem.at[0]),
        pltpu.make_async_copy(f_hbm, f_v, local_sem.at[1]),
        pltpu.make_async_copy(g_hbm, g_v, local_sem.at[2]),
        pltpu.make_async_copy(ct_hbm, ct_v, local_sem.at[3]),
    ]
    for load in loads:
        load.start()

    y_right, y_left = dev(xh, xl, turn(y, 1), z, c), dev(xh, xl, turn(y, -1), z, c)
    z_right, z_left = dev(xh, xl, y, turn(z, 1), c), dev(xh, xl, y, turn(z, -1), c)
    sibling = dev(xh, xl, y, z, oc)
    h_partner = dev(oh, xl, y, z, c)
    l_partner = dev(xh, ox, y, z, c)
    place = 2 * xh + xl
    x_up, x_down = lax.rem(place + 1, 4), lax.rem(place + 3, 4)
    x_right = dev(x_up // 2, lax.rem(x_up, 2), y, z, c)
    x_left = dev(x_down // 2, lax.rem(x_down, 2), y, z, c)

    barrier = pltpu.get_barrier_semaphore()
    peers = [y_right, y_left, sibling]
    peers += [dev(xh, xl, y, turn(z, by), c) for by in range(1, 8)]
    for by in range(1, 4):
        other = lax.rem(place + by, 4)
        peers.append(dev(other // 2, lax.rem(other, 2), y, z, c))
    for peer in peers:
        pl.semaphore_signal(barrier, inc=1, device_id=peer, device_id_type=MESH)

    own_tok = tok_ref[...]
    tokb[xh, y, c] = own_tok

    @pl.when(y == z)
    def _():
        tb[xh, c, xl, z] = own_tok

    lane = lax.broadcasted_iota(jnp.int32, (64, 128), 1)
    low64 = lane < 64
    low128 = lax.broadcasted_iota(jnp.int32, (128, 128), 1) < 64

    def flip(v):
        return pltpu.roll(v, 64, 1)

    def fold_low(v, h):
        top, bottom = v[:64], v[64:]
        return jnp.where(low64, top, flip(bottom)) if h == 0 else jnp.where(low64, flip(top), bottom)

    def fold_high(v, h):
        top, bottom = v[:64], v[64:]
        return jnp.where(low64, bottom, flip(top)) if h == 0 else jnp.where(low64, flip(bottom), top)

    go = go_ref[...].astype(F32)
    taps = taps_ref[...]
    packs = [
        jnp.concatenate([fold_high(go, h), fold_low(taps, h)], axis=0).astype(BF16)
        for h in range(2)
    ]
    first = xl == 0
    gtb[z, xl] = jnp.where(first, packs[0], packs[1])
    gtx[...] = jnp.where(first, packs[1], packs[0])

    pl.semaphore_wait(barrier, len(peers))

    ring_a = Ring(lambda q: tokb.at[xh, q, c], half_of(128), y, y_right, y_left, ra_s, ra_r)
    ring_b = Ring(lambda q: tokb.at[oh, q, c], half_of(128), y, y_right, y_left, rb_s, rb_r)
    gate_a = Ring(lambda q: gtb.at[q, xl], half_of(128), z, z_right, z_left, ga_s, ga_r)
    gate_b = Ring(lambda q: gtb.at[q, ox], half_of(128), z, z_right, z_left, gb_s, gb_r)
    proj_a = Ring(lambda q: qvb.at[q, xl], half_of(192), z, z_right, z_left, qa_s, qa_r)
    proj_b = Ring(lambda q: qvb.at[q, ox], half_of(192), z, z_right, z_left, qb_s, qb_r)

    def sib_copy(side, index, away, core):
        ref = tokb.at[xh if side == 0 else oh, turn(y, away), core]
        return remote(ref, ref, sib_s.at[side, index], sib_r.at[side, index], sibling)

    index_of = {0: 0, -1: 1, -2: 2, -3: 3, 4: 4, 1: 5, 2: 6, 3: 7}

    def to_sibling(side, aways):
        for away in aways:
            sib_copy(side, index_of[away], away, c).start()

    tok_pair_out = remote(tokb.at[xh, y, c], tokb.at[xh, y, c], pair_s.at[0], pair_r.at[0], h_partner)
    tok_pair_in = remote(tokb.at[oh, y, c], tokb.at[oh, y, c], pair_s.at[0], pair_r.at[0], h_partner)
    gate_out = remote(gtx, gtb.at[z, xl], pair_s.at[1], pair_r.at[1], l_partner)
    gate_in = remote(gtx, gtb.at[z, ox], pair_s.at[1], pair_r.at[1], l_partner)
    proj_out = remote(qvx, qvb.at[z, xl], pair_s.at[2], pair_r.at[2], l_partner)
    proj_in = remote(qvx, qvb.at[z, ox], pair_s.at[2], pair_r.at[2], l_partner)

    tok_pair_out.start()
    ring_a.send(1)
    to_sibling(0, [0])
    gate_out.start()
    gate_a.send(1)
    turn_own = tb.at[xh, c, xl, z]
    turn_out = remote(tokb.at[xh, y, c], turn_own, tr_s.at[0], tr_r.at[z], dev(xh, xl, y, y, c))

    @pl.when(y != z)
    def _():
        turn_out.start()

    tok_pair_in.wait_recv()
    ring_b.send(1)
    to_sibling(1, [0])
    gate_in.wait_recv()
    gate_b.send(1)
    acc[...] = jnp.zeros_like(acc)
    loads[0].wait()

    def project(away):
        for side in range(2):
            sib_copy(side, index_of[away], away, oc).wait_recv()
            q = turn(y, away)
            h = xh if side == 0 else oh
            left = jnp.concatenate([tokb[h, q, 0], tokb[h, q, 1]], axis=1)
            rows = pl.ds(pl.multiple_of((h * 8 + q) * 256, 256), 256)
            right = jnp.concatenate([w_v[j, rows, :] for j in range(3)], axis=1)
            acc[...] += jnp.dot(left, right, preferred_element_type=F32)

    for step in range(1, 5):
        new = [-step, step] if step < 4 else [4]
        for side, ring in ((0, ring_a), (1, ring_b)):
            ring.wait(step)
            if step < 4:
                ring.send(step + 1)
            to_sibling(side, new)
        for ring in (gate_a, gate_b):
            ring.wait(step)
            if step < 4:
                ring.send(step + 1)
        for away in [0] if step == 1 else [1 - step, step - 1]:
            project(away)
    project(4)

    projected = acc[...].astype(BF16).astype(F32)
    qp, kp, vp = projected[:, :128], projected[:, 128:256], projected[:, 256:]
    both = []
    for h in range(2):
        kq = jnp.where(low128, kp, flip(qp)) if h == 0 else jnp.where(low128, flip(kp), qp)
        both.append(jnp.concatenate([kq, fold_low(vp, h)], axis=0).astype(BF16))
    qvx[...] = jnp.where(first, both[1], both[0])
    proj_out.start()
    qvb[z, xl] = jnp.where(first, both[0], both[1])
    proj_a.send(1)


    d = turn(y, -z)
    dist = jnp.where(d <= 4, d, 8 - d)
    goes_right = d <= 3
    goes_left = jnp.logical_or(d == 0, d >= 6)
    up_h, up_l = x_up // 2, lax.rem(x_up, 2)
    down_h, down_l = x_down // 2, lax.rem(x_down, 2)

    def block_of(h, core, l, k):
        return tb.at[h, core, l, pl.ds(2 * k, 2)]

    def along_y(way, k):
        ref = block_of(xh, c, xl, k)
        return remote(ref, ref, ty_s.at[way, k], ty_r.at[k], y_right if way == 0 else y_left)

    def along_x(way, k):
        ref = block_of(xh, c, xl, k)
        return remote(ref, ref, tx_s.at[way, k], tx_r.at[way, k], x_right if way == 0 else x_left)

    def from_x(way, k):
        ref = block_of(down_h, c, down_l, k) if way == 0 else block_of(up_h, c, up_l, k)
        return remote(ref, ref, tx_s.at[way, k], tx_r.at[way, k], x_right if way == 0 else x_left)

    def half_on(way, k):
        h, l = (down_h, down_l) if way == 0 else (up_h, up_l)
        ref = tb.at[h, c, l, 2 * k + way]
        return remote(ref, ref, tx2_s.at[way, k], tx2_r.at[way, k], x_right if way == 0 else x_left)

    def half_from(way, k):
        ref = tb.at[oh, c, xl, 2 * k + way]
        return remote(ref, ref, tx2_s.at[way, k], tx2_r.at[way, k], x_right if way == 0 else x_left)

    piece_at = [(xh, xl), (down_h, down_l), (up_h, up_l), (oh, xl)]

    def t_sibling(piece, k, core):
        h, l = piece_at[piece]
        ref = block_of(h, core, l, k)
        return remote(ref, ref, ts_s.at[piece, k], ts_r.at[piece, k], sibling)

    def slot(tau):
        k = tau - dist

        @pl.when(jnp.logical_and(k >= 0, k < CHUNKS))
        def _():
            @pl.when(d != 0)
            def _():
                along_y(0, k).wait_recv()

            @pl.when(goes_right)
            def _():
                along_y(0, k).start()

            @pl.when(goes_left)
            def _():
                along_y(1, k).start()

            along_x(0, k).start()
            along_x(1, k).start()
            t_sibling(0, k, c).start()

        m = k - 1

        @pl.when(jnp.logical_and(m >= 0, m < CHUNKS))
        def _():
            from_x(0, m).wait_recv()
            half_on(0, m).start()
            from_x(1, m).wait_recv()
            half_on(1, m).start()
            t_sibling(1, m, c).start()
            t_sibling(2, m, c).start()

        n = k - 2

        @pl.when(jnp.logical_and(n >= 0, n < CHUNKS))
        def _():
            half_from(0, n).wait_recv()
            half_from(1, n).wait_recv()
            t_sibling(3, n, c).start()

    @pl.when(d == 0)
    def _():
        for by in range(1, 8):
            source = turn(z, by)
            ref = tb.at[xh, c, xl, source]
            remote(ref, ref, tr_s.at[0], tr_r.at[source], sibling).wait_recv()

    slot(0)
    proj_in.wait_recv()
    proj_b.send(1)


    def put_spectra(x, rows_lo, rows_hi):
        spectra = real_forward(32, x)
        yb[0, rows_lo, :] = spectra[0][0].astype(BF16)
        yb[0, rows_hi, :] = spectra[16][0].astype(BF16)
        for k in range(1, 16):
            yb[k, rows_lo, :] = spectra[k][0].astype(BF16)
            yb[k, rows_hi, :] = spectra[k][1].astype(BF16)

    low16 = lax.broadcasted_iota(jnp.int32, (16, 128), 1) < 64

    def rows_at(start):
        return pl.ds(pl.multiple_of(start, 16), 16)

    def filter_rows(i, carry):
        top, bottom = [], []
        for a in range(16):
            packed = gtb[a % 8, a // 8, rows_at(64 + 16 * i), :].astype(F32)
            turned = flip(packed)
            top.append(jnp.where(low16, packed, turned))
            bottom.append(jnp.where(low16, turned, packed))
        put_spectra(top, rows_at(16 * i), rows_at(128 + 16 * i))
        put_spectra(bottom, rows_at(64 + 16 * i), rows_at(192 + 16 * i))
        return carry

    lax.fori_loop(0, 4, filter_rows, 0)
    loads[1].wait()
    row0 = lax.broadcasted_iota(jnp.int32, (128, 128), 0) == 0

    def filter_tile(k, carry):
        spec = jnp.dot(f_v[k], yb[k], preferred_element_type=F32)
        fs[k, :128, :] = spec[:128]
        im = spec[128:]
        special = jnp.logical_and(row0, k == 0)
        fs[k, 128:, :] = jnp.where(jnp.logical_or(low128, special), im, -im)
        return carry

    lax.fori_loop(0, 16, filter_tile, 0)

    for step in range(1, 5):
        for ring in (proj_a, proj_b):
            ring.wait(step)
            if step < 4:
                ring.send(step + 1)
        slot(step)


    def field_rows(i, carry):
        top, bottom = [], []
        for a in range(16):
            za, la = a % 8, a // 8
            vals = qvb[za, la, rows_at(128 + 16 * i), :].astype(F32)
            gos = gtb[za, la, rows_at(16 * i), :].astype(F32)
            b_top = jnp.where(low16, vals, gos)
            b_bottom = flip(jnp.where(low16, gos, vals))
            bv[a, rows_at(16 * i), :] = b_top.astype(BF16)
            bv[a, rows_at(64 + 16 * i), :] = b_bottom.astype(BF16)
            top.append(qvb[za, la, rows_at(16 * i), :].astype(F32) * b_top)
            bottom.append(qvb[za, la, rows_at(64 + 16 * i), :].astype(F32) * b_bottom)
        put_spectra(top, rows_at(16 * i), rows_at(128 + 16 * i))
        put_spectra(bottom, rows_at(64 + 16 * i), rows_at(192 + 16 * i))
        return carry

    lax.fori_loop(0, 4, field_rows, 0)
    slot(5)
    loads[2].wait()

    def mix_tile(k, carry):
        spec = jnp.dot(f_v[k], yb[k], preferred_element_type=F32)
        sr, si = spec[:128], spec[128:]
        fr, fi = fs[k, :128, :], fs[k, 128:, :]
        tr, ti = flip(sr), flip(si)
        special = jnp.logical_and(row0, k == 0)
        mixed_re = jnp.where(special, fr * sr, fr * sr - fi * si)
        mixed_im = jnp.where(special, fi * si, fr * si + fi * sr)
        grad_re = jnp.where(special, tr * sr, tr * sr + ti * si)
        grad_im = jnp.where(special, ti * si, ti * sr - tr * si)
        mixed = jnp.concatenate(
            [
                jnp.concatenate([mixed_re, grad_re], axis=1),
                jnp.concatenate([mixed_im, grad_im], axis=1),
            ],
            axis=0,
        ).astype(BF16)
        zb[k] = jnp.dot(g_v[k], mixed, preferred_element_type=F32)
        return carry

    lax.fori_loop(0, 16, mix_tile, 0)
    slot(6)


    def back_rows(i, carry):
        lo, hi = rows_at(16 * i), rows_at(128 + 16 * i)
        spectra = [(zb[0, lo, :128], None)]
        spectra += [(zb[k, lo, :128], zb[k, hi, :128]) for k in range(1, 16)]
        spectra += [(zb[0, hi, :128], None)]
        for a, restored in enumerate(real_inverse(32, spectra, half=True)):
            turned = flip(restored)
            out = rows_at(128 * a + 16 * i)
            gp[out, :128] = (turned * bv[a, lo, :].astype(F32)).astype(BF16)
            gp[out, 128:] = (turned * qvb[a % 8, a // 8, lo, :].astype(F32)).astype(BF16)
        return carry

    lax.fori_loop(0, 8, back_rows, 0)
    slot(7)
    slot(8)
    slot(9)


    for piece in range(4):
        for k in range(CHUNKS):
            t_sibling(piece, k, oc).wait_recv()

    def weight_rows(h, core):
        lhs = tb[h, core].reshape(2048, 128)
        return lax.dot_general(lhs, gp[...], (((0,), (0,)), ((), ())), preferred_element_type=F32)

    away_parts = [weight_rows(ox, core) for core in range(2)]
    for core in range(2):
        rsend[core * 128 : core * 128 + 128, :] = away_parts[core][:, :128].astype(BF16)
    rsend[256:, :] = jnp.where(low128, away_parts[0][:, 128:], flip(away_parts[1][:, 128:])).astype(BF16)
    weight_out = remote(rsend, rrecv, pair_s.at[3], pair_r.at[3], l_partner)
    weight_out.start()

    loads[3].wait()

    def filter_grad_step(k, carry):
        sums = []
        for l in range(2):
            block = z + 8 * l
            total = carry[l] + ct_v[block, pl.ds(k, 1), :] * zb[k, :128, 128:]
            sums.append(total + ct_v[block, pl.ds(k + 16, 1), :] * zb[k, 128:, 128:])
        return tuple(sums)

    zero = jnp.zeros((128, 128), F32)
    near, far = lax.fori_loop(0, 16, filter_grad_step, (zero, zero))
    own = jnp.where(first, near, far)
    other = jnp.where(first, far, near)
    fsend[...] = jnp.where(low64, other[:64], flip(other[64:]))
    filter_out = remote(fsend, frecv, pair_s.at[4], pair_r.at[4], l_partner)
    filter_out.start()
    fown[...] = own

    for core in range(2):
        rown[core * 128 : core * 128 + 128, :] = weight_rows(xl, core)

    def unfolded(mine, got):
        turned, turned_mine = flip(got), flip(mine)
        low = lax.broadcasted_iota(jnp.int32, mine.shape, 1) < 64
        as_first = jnp.where(low, mine, jnp.concatenate([turned, got], axis=0))
        as_second = jnp.where(low, jnp.concatenate([got, turned], axis=0), turned_mine)
        return jnp.where(first, as_first, as_second)

    weight_out.wait_recv()
    mine = rown[:, :128]
    got = rrecv[:256, :].astype(F32)
    mine_turned, got_turned = flip(mine), flip(got)
    low256 = lax.broadcasted_iota(jnp.int32, (256, 128), 1) < 64
    wg_ref[0] = jnp.where(
        first, jnp.where(low256, mine_turned, got), jnp.where(low256, got_turned, mine)
    )
    wg_ref[1] = jnp.where(
        first, jnp.where(low256, mine, got_turned), jnp.where(low256, got, mine_turned)
    )
    wg_ref[2] = unfolded(rown[:, 128:], rrecv[256:, :].astype(F32))
    filter_out.wait_recv()
    fg_ref[...] = unfolded(fown[...], frecv[...])

    for ring in (ring_a, ring_b, gate_a, gate_b, proj_a, proj_b):
        ring.drain()
    for sent in (tok_pair_out, gate_out, proj_out, weight_out, filter_out):
        sent.wait_send()
    for side in range(2):
        for away, index in index_of.items():
            sib_copy(side, index, away, c).wait_send()

    @pl.when(y != z)
    def _():
        turn_out.wait_send()

    for k in range(CHUNKS):

        @pl.when(goes_right)
        def _():
            along_y(0, k).wait_send()

        @pl.when(goes_left)
        def _():
            along_y(1, k).wait_send()

        for way in range(2):
            along_x(way, k).wait_send()
            half_on(way, k).wait_send()
        for piece in range(4):
            t_sibling(piece, k, c).wait_send()


def on_device(tables, tokens, in_weight, filter_taps, grad_out):
    forward, inverse, single = tables
    vmem = pl.BlockSpec(memory_space=pltpu.VMEM)
    anywhere = pl.BlockSpec(memory_space=pl.ANY)
    dma = pltpu.SemaphoreType.DMA
    ring_sems = [dma((2, 4)) for _ in range(12)]
    weight_grad, filter_grad = pl.pallas_call(
        kernel,
        out_shape=(
            jax.ShapeDtypeStruct((3, 256, 128), F32),
            jax.ShapeDtypeStruct((128, 128), F32),
        ),
        in_specs=[vmem] * 3 + [anywhere] * 4,
        out_specs=(vmem, vmem),
        scratch_shapes=[
            pltpu.VMEM((3, 4096, 128), BF16),
            pltpu.VMEM((16, 256, 256), BF16),
            pltpu.VMEM((16, 256, 256), BF16),
            pltpu.VMEM((16, 32, 128), F32),
            pltpu.VMEM((2, 8, 2, 128, 128), BF16),
            pltpu.VMEM((8, 2, 128, 128), BF16),
            pltpu.VMEM((128, 128), BF16),
            pltpu.VMEM((8, 2, 192, 128), BF16),
            pltpu.VMEM((192, 128), BF16),
            pltpu.VMEM((2, 2, 2, 8, 128, 128), BF16),
            pltpu.VMEM((128, 384), F32),
            pltpu.VMEM((16, 128, 128), BF16),
            pltpu.VMEM((16, 256, 128), BF16),
            pltpu.VMEM((16, 256, 128), F32),
            pltpu.VMEM((16, 256, 256), F32),
            pltpu.VMEM((2048, 256), BF16),
            pltpu.VMEM((256, 256), F32),
            pltpu.VMEM((384, 128), BF16),
            pltpu.VMEM((384, 128), BF16),
            pltpu.VMEM((128, 128), F32),
            pltpu.VMEM((64, 128), F32),
            pltpu.VMEM((64, 128), F32),
            dma((4,)),
            *ring_sems,
            dma((5,)), dma((5,)),
            dma((2, 8)), dma((2, 8)),
            dma((1,)), dma((8,)),
            dma((2, CHUNKS)), dma((CHUNKS,)),
            dma((2, CHUNKS)), dma((2, CHUNKS)),
            dma((2, CHUNKS)), dma((2, CHUNKS)),
            dma((4, CHUNKS)), dma((4, CHUNKS)),
        ],
        compiler_params=pltpu.CompilerParams(
            collective_id=0, has_side_effects=True, vmem_limit_bytes=52 * 1024 * 1024
        ),
        cost_estimate=pl.CostEstimate(flops=3_000_000_000, bytes_accessed=10_000_000, transcendentals=0),
    )(
        tokens,
        grad_out,
        filter_taps,
        jnp.transpose(in_weight, (1, 0, 2)),
        forward,
        inverse,
        single,
    )
    return jnp.transpose(weight_grad, (1, 0, 2)), filter_grad


def solution(mesh):
    tables = transform_tables()

    def whole(tokens, in_weight, filter_taps, grad_out):
        constants = tuple(jnp.asarray(t) for t in tables)
        placed = (P("ctx", "ch"), P(None, None, "ch"), P("ctx", "ch"), P("ctx", "ch"))
        return jax.shard_map(
            on_device,
            mesh=mesh,
            in_specs=((P(), P(), P()),) + placed,
            out_specs=(P("ctx", None, "ch"), P("ctx", "ch")),
            check_vma=False,
        )(constants, tokens, in_weight, filter_taps, grad_out)

    return whole
```

time: 349 us -> 85.3 us (0.24)
  the two profiles are of different devices: /device:TPU:24 before, /device:TPU:33 now
where the time goes in v1:
time: 85.3 us; the launch traced here: 85 us
  Pallas kernels  79.7 us (93%)
  local copies, waits for them, and re-layouts  4.67 us (5%)
    pallas_call x1, Pallas kernels, on_device(): pl.pallas_call(kernel, out_shape=(jax.ShapeDtypeStruct((3, 256, 128), F32...  79.7 us
    unnamed x10, local copies, waits for them, and re-layouts  4.67 us

profile of v1, /device:TPU:33, one launch (start us, length us, event | category | flops | bytes accessed | tf_op | source)
XLA Modules:
  0.0 85.0 jit_solution(16750982491954167885)
XLA Ops:
  0.6 0.0 copy-start
  0.6 0.8 copy-done
  1.5 0.0 copy-start.1
  1.5 0.8 copy-done.1
  2.2 0.0 copy-start.2
  2.2 0.8 copy-done.2
  3.0 0.0 copy-start.3
  3.0 0.9 %copy-done.3 = f32[16,32,128]{2,1,0:T(8,128)S(1)} copy-done((f32[16,32,128]{2,1,0:T(8,128)S(1)}, f32[16,32,128]{2,1,0:T(8,128)}, u32[]{:S(2)}) %copy-start.3) | copy-done | bytes 262168
  3.9 79.7 %shard_map.86 = (f32[3,256,128]{2,1,0:T(8,128)S(1)}, f32[128,128]{1,0:T(8,128)S(1)}) custom-call(bf16[128,128]{1,0:T(8,128)(2,1)S(1)} %copy-done.1, bf16[128,128]{1,0:T(8,128)(2,1)S(1)} %copy-done.2, f32[128,128]{1,0:T(8,128)S(1)} %copy-done, bf16[3,4096,128]{2,1,0:T(8,128)(2,1)} %bitcast.3, bf16[16,256,256]{2,1,0:T(8,128)(2,1)} %constant.6.clone.f_hbm, ...), custom_call_target="tpu_custom_call" | custom-call | flops 3000000000 | bytes 10000000 | tf_op jit(solution)/shard_map/pallas_call | solution.py:647
  83.6 0.7 copy.11
  84.4 0.6 copy.12
Async XLA Ops:
  0.6 0.8 copy-start
  1.5 0.8 copy-start.1
  2.2 0.8 copy-start.2
  3.0 0.9 %copy-start.3 = (f32[16,32,128]{2,1,0:T(8,128)S(1)}, f32[16,32,128]{2,1,0:T(8,128)}, u32[]{:S(2)}) copy-start(f32[16,32,128]{2,1,0:T(8,128)} %constant.8.clone.ct_hbm) | copy-start | bytes 786436

commit v2 on v1

--- a/solution.py
+++ b/solution.py
@@ -14,7 +14,8 @@
 F32 = jnp.float32
 ROWS = 128
 TILES = 16
-CHUNKS = 4
+CHUNKS = 2
+PER = 8 // CHUNKS
 
 
 def transform_tables():
@@ -139,59 +140,65 @@
     return low if half else low + [even[a] - odd[a] for a in range(h)]
 
 
-class Ring:
-    def __init__(self, slot, half, place, right, left, send_sem, recv_sem):
-        self.slot, self.half, self.place = slot, half, place
-        self.to = (right, left)
+class Spread:
+    NAMES = {(-1, None): 0, (-2, None): 1, (-3, None): 2, (-4, 0): 3, (-4, 1): 4, (3, None): 5, (2, None): 6, (1, None): 7}
+
+    def __init__(self, slot, rows, place, to, send_sem, recv_sem):
+        self.slot, self.rows, self.place, self.to = slot, rows, place, to
         self.send_sem, self.recv_sem = send_sem, recv_sem
-
-    def at(self, away):
-        return lax.rem(self.place + 8 + away, 8)
-
-    def copy(self, ref, way, step):
+        self.sent = []
+
+    def copy(self, ref, name, device):
+        if name[1] is not None:
+            ref = ref.at[pl.ds(name[1] * (self.rows // 2), self.rows // 2)]
+        at = self.NAMES[name]
         return pltpu.make_async_remote_copy(
-            src_ref=ref,
-            dst_ref=ref,
-            send_sem=self.send_sem.at[way, step - 1],
-            recv_sem=self.recv_sem.at[way, step - 1],
-            device_id=self.to[way],
-            device_id_type=MESH,
+            src_ref=ref, dst_ref=ref, send_sem=self.send_sem.at[at], recv_sem=self.recv_sem.at[at],
+            device_id=device, device_id_type=MESH,
         )
 
-    def sent(self, way, step):
-        away = (1 - step) if way == 0 else (step - 1)
-        ref = self.slot(self.at(away))
-        return self.copy(self.half(ref, way) if step == 4 else ref, way, step)
-
-    def send(self, step):
-        for way in range(2):
-            self.sent(way, step).start()
-
-    def wait(self, step):
-        for way in range(2):
-            ref = self.slot(self.at(-step if way == 0 else step))
-            self.copy(self.half(ref, way) if step == 4 else ref, way, step).wait_recv()
+    def send(self, origin, distance, half=None):
+        seen = origin - distance
+        name = (-4 if seen == 4 else seen, half)
+        copy = self.copy(self.slot(lax.rem(self.place + 8 + origin, 8)), name, self.to(distance))
+        copy.start()
+        self.sent.append(copy)
+
+    def wait(self, origin, half=None):
+        self.copy(self.slot(lax.rem(self.place + 8 + origin, 8)), (origin, half), self.to(1)).wait_recv()
+
+    def first(self):
+        for distance in (2, -2, 1, -1):
+            self.send(0, distance)
+
+    def middle(self):
+        self.wait(-2)
+        self.send(-2, 2, 0)
+        self.send(-2, 1)
+        self.wait(2)
+        self.send(2, -2, 1)
+        self.send(2, -1)
+        self.wait(-1)
+        self.wait(1)
+
+    def last(self):
+        self.wait(-3)
+        self.wait(3)
+        self.wait(-4, 0)
+        self.wait(-4, 1)
 
     def drain(self):
-        for step in range(1, 5):
-            for way in range(2):
-                self.sent(way, step).wait_send()
-
-
-def half_of(rows):
-    def half(ref, way):
-        return ref.at[pl.ds(way * (rows // 2), rows // 2)]
-
-    return half
+        for copy in self.sent:
+            copy.wait_send()
 
 
 def kernel(
-    tok_ref, go_ref, taps_ref, w_hbm, f_hbm, g_hbm, ct_hbm,
+    tok_hbm, go_hbm, taps_hbm, w_hbm, f_hbm, g_hbm, ct_hbm,
     wg_ref, fg_ref,
-    w_v, f_v, g_v, ct_v, tokb, gtb, gtx, qvb, qvx, tb, acc, bv, yb, fs, zb, gp,
+    go_v, taps_v, w_v, f_v, g_v, ct_v, tokb, gtb, gtx, qvb, qvx, tb, acc, bv, yb, fs, zb, gp,
     rown, rsend, rrecv, fown, fsend, frecv,
     local_sem, ra_s, ra_r, rb_s, rb_r, ga_s, ga_r, gb_s, gb_r, qa_s, qa_r, qb_s, qb_r,
-    pair_s, pair_r, sib_s, sib_r, tr_s, tr_r, ty_s, ty_r, tx_s, tx_r, tx2_s, tx2_r, ts_s, ts_r,
+    pair_s, pair_r, sib_s, sib_r, tr_s, tr_r, tx_s, tx_r, tx2_s, tx2_r, ts_s, ts_r,
 ):
     ctx, ch = lax.axis_index("ctx"), lax.axis_index("ch")
     xl, z = ctx // 8, lax.rem(ctx, 8)
@@ -209,6 +216,35 @@
     def turn(v, by):
         return lax.rem(v + 8 + by, 8)
 
+    def along(axis):
+        if axis == "y":
+            return lambda by: dev(xh, xl, turn(y, by), z, c)
+        return lambda by: dev(xh, xl, y, turn(z, by), c)
+
+    sibling = dev(xh, xl, y, z, oc)
+    h_partner = dev(oh, xl, y, z, c)
+    l_partner = dev(xh, ox, y, z, c)
+    place = 2 * xh + xl
+    x_up, x_down = lax.rem(place + 1, 4), lax.rem(place + 3, 4)
+    x_right = dev(x_up // 2, lax.rem(x_up, 2), y, z, c)
+    x_left = dev(x_down // 2, lax.rem(x_down, 2), y, z, c)
+
+    barrier = pltpu.get_barrier_semaphore()
+    peers = [sibling] + [along("y")(by) for by in (-2, -1, 1, 2)]
+    peers += [along("z")(by) for by in range(1, 8)]
+    for by in range(1, 4):
+        other = lax.rem(place + by, 4)
+        peers.append(dev(other // 2, lax.rem(other, 2), y, z, c))
+    for peer in peers:
+        pl.semaphore_signal(barrier, inc=1, device_id=peer, device_id_type=MESH)
+
+    own_loads = [
+        pltpu.make_async_copy(go_hbm, go_v, local_sem.at[4]),
+        pltpu.make_async_copy(taps_hbm, taps_v, local_sem.at[5]),
+        pltpu.make_async_copy(tok_hbm, tokb.at[xh, y, c], local_sem.at[6]),
+    ]
+    for load in own_loads:
+        load.start()
     loads = [
         pltpu.make_async_copy(w_hbm, w_v, local_sem.at[0]),
         pltpu.make_async_copy(f_hbm, f_v, local_sem.at[1]),
@@ -218,32 +254,6 @@
     for load in loads:
         load.start()
 
-    y_right, y_left = dev(xh, xl, turn(y, 1), z, c), dev(xh, xl, turn(y, -1), z, c)
-    z_right, z_left = dev(xh, xl, y, turn(z, 1), c), dev(xh, xl, y, turn(z, -1), c)
-    sibling = dev(xh, xl, y, z, oc)
-    h_partner = dev(oh, xl, y, z, c)
-    l_partner = dev(xh, ox, y, z, c)
-    place = 2 * xh + xl
-    x_up, x_down = lax.rem(place + 1, 4), lax.rem(place + 3, 4)
-    x_right = dev(x_up // 2, lax.rem(x_up, 2), y, z, c)
-    x_left = dev(x_down // 2, lax.rem(x_down, 2), y, z, c)
-
-    barrier = pltpu.get_barrier_semaphore()
-    peers = [y_right, y_left, sibling]
-    peers += [dev(xh, xl, y, turn(z, by), c) for by in range(1, 8)]
-    for by in range(1, 4):
-        other = lax.rem(place + by, 4)
-        peers.append(dev(other // 2, lax.rem(other, 2), y, z, c))
-    for peer in peers:
-        pl.semaphore_signal(barrier, inc=1, device_id=peer, device_id_type=MESH)
-
-    own_tok = tok_ref[...]
-    tokb[xh, y, c] = own_tok
-
-    @pl.when(y == z)
-    def _():
-        tb[xh, c, xl, z] = own_tok
-
     lane = lax.broadcasted_iota(jnp.int32, (64, 128), 1)
     low64 = lane < 64
     low128 = lax.broadcasted_iota(jnp.int32, (128, 128), 1) < 64
@@ -259,8 +269,10 @@
         top, bottom = v[:64], v[64:]
         return jnp.where(low64, bottom, flip(top)) if h == 0 else jnp.where(low64, flip(bottom), top)
 
-    go = go_ref[...].astype(F32)
-    taps = taps_ref[...]
+    for load in own_loads:
+        load.wait()
+    go = go_v[...].astype(F32)
+    taps = taps_v[...]
     packs = [
         jnp.concatenate([fold_high(go, h), fold_low(taps, h)], axis=0).astype(BF16)
         for h in range(2)
@@ -271,18 +283,18 @@
 
     pl.semaphore_wait(barrier, len(peers))
 
-    ring_a = Ring(lambda q: tokb.at[xh, q, c], half_of(128), y, y_right, y_left, ra_s, ra_r)
-    ring_b = Ring(lambda q: tokb.at[oh, q, c], half_of(128), y, y_right, y_left, rb_s, rb_r)
-    gate_a = Ring(lambda q: gtb.at[q, xl], half_of(128), z, z_right, z_left, ga_s, ga_r)
-    gate_b = Ring(lambda q: gtb.at[q, ox], half_of(128), z, z_right, z_left, gb_s, gb_r)
-    proj_a = Ring(lambda q: qvb.at[q, xl], half_of(192), z, z_right, z_left, qa_s, qa_r)
-    proj_b = Ring(lambda q: qvb.at[q, ox], half_of(192), z, z_right, z_left, qb_s, qb_r)
+    tok_a = Spread(lambda q: tokb.at[xh, q, c], 128, y, along("y"), ra_s, ra_r)
+    tok_b = Spread(lambda q: tokb.at[oh, q, c], 128, y, along("y"), rb_s, rb_r)
+    gate_a = Spread(lambda q: gtb.at[q, xl], 128, z, along("z"), ga_s, ga_r)
+    gate_b = Spread(lambda q: gtb.at[q, ox], 128, z, along("z"), gb_s, gb_r)
+    proj_a = Spread(lambda q: qvb.at[q, xl], 192, z, along("z"), qa_s, qa_r)
+    proj_b = Spread(lambda q: qvb.at[q, ox], 192, z, along("z"), qb_s, qb_r)
 
     def sib_copy(side, index, away, core):
         ref = tokb.at[xh if side == 0 else oh, turn(y, away), core]
         return remote(ref, ref, sib_s.at[side, index], sib_r.at[side, index], sibling)
 
-    index_of = {0: 0, -1: 1, -2: 2, -3: 3, 4: 4, 1: 5, 2: 6, 3: 7}
+    index_of = {0: 0, -1: 1, -2: 2, -3: 3, -4: 4, 3: 5, 2: 6, 1: 7}
 
     def to_sibling(side, aways):
         for away in aways:
@@ -295,52 +307,67 @@
     proj_out = remote(qvx, qvb.at[z, xl], pair_s.at[2], pair_r.at[2], l_partner)
     proj_in = remote(qvx, qvb.at[z, ox], pair_s.at[2], pair_r.at[2], l_partner)
 
+    def turn_copy(away):
+        q = turn(y, away)
+        return remote(
+            tokb.at[xh, q, c], tb.at[xh, c, xl, z], tr_s.at[index_of[away]], tr_r.at[z], dev(xh, xl, y, q, c)
+        )
+
+    def turned_over(aways):
+        for away in aways:
+            q = turn(y, away)
+
+            @pl.when(q == z)
+            def _():
+                tb[xh, c, xl, z] = tokb[xh, q, c]
+
+            @pl.when(q != z)
+            def _():
+                turn_copy(away).start()
+
+    def project(aways):
+        total = None
+        for away in aways:
+            for side in range(2):
+                sib_copy(side, index_of[away], away, oc).wait_recv()
+                q = turn(y, away)
+                h = xh if side == 0 else oh
+                left = jnp.concatenate([tokb[h, q, 0], tokb[h, q, 1]], axis=1)
+                rows = pl.ds(pl.multiple_of((h * 8 + q) * 256, 256), 256)
+                right = jnp.concatenate([w_v[j, rows, :] for j in range(3)], axis=1)
+                term = jnp.dot(left, right, preferred_element_type=F32)
+                total = term if total is None else total + term
+        return total
+
     tok_pair_out.start()
-    ring_a.send(1)
+    tok_a.first()
     to_sibling(0, [0])
     gate_out.start()
-    gate_a.send(1)
-    turn_own = tb.at[xh, c, xl, z]
-    turn_out = remote(tokb.at[xh, y, c], turn_own, tr_s.at[0], tr_r.at[z], dev(xh, xl, y, y, c))
-
-    @pl.when(y != z)
-    def _():
-        turn_out.start()
-
+    gate_a.first()
+    turned_over([0])
     tok_pair_in.wait_recv()
-    ring_b.send(1)
+    tok_b.first()
     to_sibling(1, [0])
     gate_in.wait_recv()
-    gate_b.send(1)
-    acc[...] = jnp.zeros_like(acc)
+    gate_b.first()
     loads[0].wait()
-
-    def project(away):
-        for side in range(2):
-            sib_copy(side, index_of[away], away, oc).wait_recv()
-            q = turn(y, away)
-            h = xh if side == 0 else oh
-            left = jnp.concatenate([tokb[h, q, 0], tokb[h, q, 1]], axis=1)
-            rows = pl.ds(pl.multiple_of((h * 8 + q) * 256, 256), 256)
-            right = jnp.concatenate([w_v[j, rows, :] for j in range(3)], axis=1)
-            acc[...] += jnp.dot(left, right, preferred_element_type=F32)
-
-    for step in range(1, 5):
-        new = [-step, step] if step < 4 else [4]
-        for side, ring in ((0, ring_a), (1, ring_b)):
-            ring.wait(step)
-            if step < 4:
-                ring.send(step + 1)
-            to_sibling(side, new)
-        for ring in (gate_a, gate_b):
-            ring.wait(step)
-            if step < 4:
-                ring.send(step + 1)
-        for away in [0] if step == 1 else [1 - step, step - 1]:
-            project(away)
-    project(4)
-
-    projected = acc[...].astype(BF16).astype(F32)
+    near, far = [-2, 2, -1, 1], [-3, 3, -4]
+    tok_a.middle()
+    to_sibling(0, near)
+    turned_over(near)
+    acc[...] = project([0])
+    tok_b.middle()
+    to_sibling(1, near)
+    gate_a.middle()
+    gate_b.middle()
+    tok_a.last()
+    to_sibling(0, far)
+    turned_over(far)
+    acc[...] += project(near)
+    tok_b.last()
+    to_sibling(1, far)
+    projected = (acc[...] + project(far)).astype(BF16).astype(F32)
+
     qp, kp, vp = projected[:, :128], projected[:, 128:256], projected[:, 256:]
     both = []
     for h in range(2):
@@ -349,22 +376,14 @@
     qvx[...] = jnp.where(first, both[1], both[0])
     proj_out.start()
     qvb[z, xl] = jnp.where(first, both[0], both[1])
-    proj_a.send(1)
-
-
-    d = turn(y, -z)
-    dist = jnp.where(d <= 4, d, 8 - d)
-    goes_right = d <= 3
-    goes_left = jnp.logical_or(d == 0, d >= 6)
+    proj_a.first()
+
+
     up_h, up_l = x_up // 2, lax.rem(x_up, 2)
     down_h, down_l = x_down // 2, lax.rem(x_down, 2)
 
     def block_of(h, core, l, k):
-        return tb.at[h, core, l, pl.ds(2 * k, 2)]
-
-    def along_y(way, k):
-        ref = block_of(xh, c, xl, k)
-        return remote(ref, ref, ty_s.at[way, k], ty_r.at[k], y_right if way == 0 else y_left)
+        return tb.at[h, core, l, pl.ds(PER * k, PER)]
 
     def along_x(way, k):
         ref = block_of(xh, c, xl, k)
@@ -376,11 +395,11 @@
 
     def half_on(way, k):
         h, l = (down_h, down_l) if way == 0 else (up_h, up_l)
-        ref = tb.at[h, c, l, 2 * k + way]
+        ref = tb.at[h, c, l, pl.ds(PER * k + PER // 2 * way, PER // 2)]
         return remote(ref, ref, tx2_s.at[way, k], tx2_r.at[way, k], x_right if way == 0 else x_left)
 
     def half_from(way, k):
-        ref = tb.at[oh, c, xl, 2 * k + way]
+        ref = tb.at[oh, c, xl, pl.ds(PER * k + PER // 2 * way, PER // 2)]
         return remote(ref, ref, tx2_s.at[way, k], tx2_r.at[way, k], x_right if way == 0 else x_left)
 
     piece_at = [(xh, xl), (down_h, down_l), (up_h, up_l), (oh, xl)]
@@ -390,56 +409,39 @@
         ref = block_of(h, core, l, k)
         return remote(ref, ref, ts_s.at[piece, k], ts_r.at[piece, k], sibling)
 
-    def slot(tau):
-        k = tau - dist
-
-        @pl.when(jnp.logical_and(k >= 0, k < CHUNKS))
-        def _():
-            @pl.when(d != 0)
-            def _():
-                along_y(0, k).wait_recv()
-
-            @pl.when(goes_right)
-            def _():
-                along_y(0, k).start()
-
-            @pl.when(goes_left)
-            def _():
-                along_y(1, k).start()
+    def round_x_first():
+        for k in range(CHUNKS):
+            for source in range(PER * k, PER * k + PER):
+                ref = tb.at[xh, c, xl, source]
+
+                @pl.when(z != source)
+                def _():
+                    remote(ref, ref, tr_s.at[0], tr_r.at[source], sibling).wait_recv()
 
             along_x(0, k).start()
             along_x(1, k).start()
             t_sibling(0, k, c).start()
 
-        m = k - 1
-
-        @pl.when(jnp.logical_and(m >= 0, m < CHUNKS))
-        def _():
-            from_x(0, m).wait_recv()
-            half_on(0, m).start()
-            from_x(1, m).wait_recv()
-            half_on(1, m).start()
-            t_sibling(1, m, c).start()
-            t_sibling(2, m, c).start()
-
-        n = k - 2
-
-        @pl.when(jnp.logical_and(n >= 0, n < CHUNKS))
-        def _():
-            half_from(0, n).wait_recv()
-            half_from(1, n).wait_recv()
-            t_sibling(3, n, c).start()
-
-    @pl.when(d == 0)
-    def _():
-        for by in range(1, 8):
-            source = turn(z, by)
-            ref = tb.at[xh, c, xl, source]
-            remote(ref, ref, tr_s.at[0], tr_r.at[source], sibling).wait_recv()
-
-    slot(0)
+    def round_x_second():
+        for k in range(CHUNKS):
+            from_x(0, k).wait_recv()
+            half_on(0, k).start()
+            from_x(1, k).wait_recv()
+            half_on(1, k).start()
+            t_sibling(1, k, c).start()
+            t_sibling(2, k, c).start()
+
+    def round_x_third():
+        for k in range(CHUNKS):
+            half_from(0, k).wait_recv()
+            half_from(1, k).wait_recv()
+            t_sibling(3, k, c).start()
+
+    round_x_first()
     proj_in.wait_recv()
-    proj_b.send(1)
+    proj_b.first()
+    gate_a.last()
+    gate_b.last()
 
 
     def put_spectra(x, rows_lo, rows_hi):
@@ -478,14 +480,13 @@
         fs[k, 128:, :] = jnp.where(jnp.logical_or(low128, special), im, -im)
         return carry
 
-    lax.fori_loop(0, 16, filter_tile, 0)
-
-    for step in range(1, 5):
-        for ring in (proj_a, proj_b):
-            ring.wait(step)
-            if step < 4:
-                ring.send(step + 1)
-        slot(step)
+    lax.fori_loop(0, 16, filter_tile, 0, unroll=16)
+
+    proj_a.middle()
+    proj_b.middle()
+    round_x_second()
+    proj_a.last()
+    proj_b.last()
 
 
     def field_rows(i, carry):
@@ -505,7 +506,6 @@
         return carry
 
     lax.fori_loop(0, 4, field_rows, 0)
-    slot(5)
     loads[2].wait()
 
     def mix_tile(k, carry):
@@ -528,8 +528,8 @@
         zb[k] = jnp.dot(g_v[k], mixed, preferred_element_type=F32)
         return carry
 
-    lax.fori_loop(0, 16, mix_tile, 0)
-    slot(6)
+    lax.fori_loop(0, 16, mix_tile, 0, unroll=16)
+    round_x_third()
 
 
     def back_rows(i, carry):
@@ -545,9 +545,6 @@
         return carry
 
     lax.fori_loop(0, 8, back_rows, 0)
-    slot(7)
-    slot(8)
-    slot(9)
 
 
     for piece in range(4):
@@ -609,28 +606,21 @@
     filter_out.wait_recv()
     fg_ref[...] = unfolded(fown[...], frecv[...])
 
-    for ring in (ring_a, ring_b, gate_a, gate_b, proj_a, proj_b):
-        ring.drain()
+    for spread in (tok_a, tok_b, gate_a, gate_b, proj_a, proj_b):
+        spread.drain()
     for sent in (tok_pair_out, gate_out, proj_out, weight_out, filter_out):
         sent.wait_send()
     for side in range(2):
         for away, index in index_of.items():
             sib_copy(side, index, away, c).wait_send()
 
-    @pl.when(y != z)
-    def _():
-        turn_out.wait_send()
+    for away in index_of:
+
+        @pl.when(turn(y, away) != z)
+        def _():
+            turn_copy(away).wait_send()
 
     for k in range(CHUNKS):
-
-        @pl.when(goes_right)
-        def _():
-            along_y(0, k).wait_send()
-
-        @pl.when(goes_left)
-        def _():
-            along_y(1, k).wait_send()
-
         for way in range(2):
             along_x(way, k).wait_send()
             half_on(way, k).wait_send()
@@ -641,18 +631,20 @@
 def on_device(tables, tokens, in_weight, filter_taps, grad_out):
     forward, inverse, single = tables
     vmem = pl.BlockSpec(memory_space=pltpu.VMEM)
-    anywhere = pl.BlockSpec(memory_space=pl.ANY)
+    anywhere = pl.BlockSpec(memory_space=pltpu.HBM)
     dma = pltpu.SemaphoreType.DMA
-    ring_sems = [dma((2, 4)) for _ in range(12)]
+    ring_sems = [dma((8,)) for _ in range(12)]
     weight_grad, filter_grad = pl.pallas_call(
         kernel,
         out_shape=(
             jax.ShapeDtypeStruct((3, 256, 128), F32),
             jax.ShapeDtypeStruct((128, 128), F32),
         ),
-        in_specs=[vmem] * 3 + [anywhere] * 4,
+        in_specs=[anywhere] * 7,
         out_specs=(vmem, vmem),
         scratch_shapes=[
+            pltpu.VMEM((128, 128), BF16),
+            pltpu.VMEM((128, 128), F32),
             pltpu.VMEM((3, 4096, 128), BF16),
             pltpu.VMEM((16, 256, 256), BF16),
             pltpu.VMEM((16, 256, 256), BF16),
@@ -675,12 +667,11 @@
             pltpu.VMEM((128, 128), F32),
             pltpu.VMEM((64, 128), F32),
             pltpu.VMEM((64, 128), F32),
-            dma((4,)),
+            dma((7,)),
             *ring_sems,
             dma((5,)), dma((5,)),
             dma((2, 8)), dma((2, 8)),
-            dma((1,)), dma((8,)),
-            dma((2, CHUNKS)), dma((CHUNKS,)),
+            dma((8,)), dma((8,)),
             dma((2, CHUNKS)), dma((2, CHUNKS)),
             dma((2, CHUNKS)), dma((2, CHUNKS)),
             dma((4, CHUNKS)), dma((4, CHUNKS)),

time: 85.3 us -> 57.9 us (0.68)
  the two profiles are of different devices: /device:TPU:33 before, /device:TPU:1 now
where the time goes in v2:
time: 57.9 us; the launch traced here: 57.6 us
  Pallas kernels  52.3 us (90%)
  local copies, waits for them, and re-layouts  4.67 us (8%)
  between operations  0.65 us (1%)
    pallas_call x1, Pallas kernels, on_device(): pl.pallas_call(kernel, out_shape=(jax.ShapeDtypeStruct((3, 256, 128), F32...  52.3 us
    unnamed x10, local copies, waits for them, and re-layouts  4.67 us

profile of v2, /device:TPU:1, one launch (start us, length us, event | category | flops | bytes accessed | tf_op | source)
XLA Modules:
  0.0 57.6 jit_solution(15377655302516210319)
XLA Ops:
  0.6 0.0 copy-start
  0.6 0.8 %copy-done = f32[128,128]{1,0:T(8,128)S(1)} copy-done((f32[128,128]{1,0:T(8,128)S(1)}, f32[128,128]{1,0:T(8,128)}, u32[]{:S(2)}) %copy-start) | copy-done | bytes 65560
  1.5 0.0 copy-start.1
  1.5 0.8 %copy-done.1 = bf16[128,128]{1,0:T(8,128)(2,1)S(1)} copy-done((bf16[128,128]{1,0:T(8,128)(2,1)S(1)}, bf16[128,128]{1,0:T(8,128)(2,1)}, u32[]{:S(2)}) %copy-start.1) | copy-done | bytes 32792
  2.2 0.0 copy-start.2
  2.2 0.8 %copy-done.2 = bf16[128,128]{1,0:T(8,128)(2,1)S(1)} copy-done((bf16[128,128]{1,0:T(8,128)(2,1)S(1)}, bf16[128,128]{1,0:T(8,128)(2,1)}, u32[]{:S(2)}) %copy-start.2) | copy-done | bytes 32792
  3.0 0.0 copy-start.3
  3.0 0.9 %copy-done.3 = f32[16,32,128]{2,1,0:T(8,128)S(1)} copy-done((f32[16,32,128]{2,1,0:T(8,128)S(1)}, f32[16,32,128]{2,1,0:T(8,128)}, u32[]{:S(2)}) %copy-start.3) | copy-done | bytes 262168
  3.9 52.3 %shard_map.86 = (f32[3,256,128]{2,1,0:T(8,128)S(1)}, f32[128,128]{1,0:T(8,128)S(1)}) custom-call(bf16[128,128]{1,0:T(8,128)(2,1)S(1)} %copy-done.1, bf16[128,128]{1,0:T(8,128)(2,1)S(1)} %copy-done.2, f32[128,128]{1,0:T(8,128)S(1)} %copy-done, bf16[3,4096,128]{2,1,0:T(8,128)(2,1)} %bitcast.3, bf16[16,256,256]{2,1,0:T(8,128)(2,1)} %constant.6.clone.f_hbm, ...), custom_call_target="tpu_custom_call" | custom-call | flops 3000000000 | bytes 10000000 | tf_op jit(solution)/shard_map/pallas_call | solution.py:637
  56.2 0.7 %copy.11 = f32[256,3,128]{2,0,1:T(8,128)} copy(f32[256,3,128]{2,0,1:T(8,128)S(1)} %bitcast.2) | data formatting | bytes 786432
  57.0 0.6 %copy.12 = f32[128,128]{1,0:T(8,128)} copy(f32[128,128]{1,0:T(8,128)S(1)} %get-tuple-element.9) | data formatting | bytes 131072
Async XLA Ops:
  0.6 0.8 %copy-start = (f32[128,128]{1,0:T(8,128)S(1)}, f32[128,128]{1,0:T(8,128)}, u32[]{:S(2)}) copy-start(f32[128,128]{1,0:T(8,128)} %taps_hbm.1) | copy-start | bytes 196612
  1.5 0.8 %copy-start.1 = (bf16[128,128]{1,0:T(8,128)(2,1)S(1)}, bf16[128,128]{1,0:T(8,128)(2,1)}, u32[]{:S(2)}) copy-start(bf16[128,128]{1,0:T(8,128)(2,1)} %tok_hbm.1) | copy-start | bytes 98308
  2.2 0.8 %copy-start.2 = (bf16[128,128]{1,0:T(8,128)(2,1)S(1)}, bf16[128,128]{1,0:T(8,128)(2,1)}, u32[]{:S(2)}) copy-start(bf16[128,128]{1,0:T(8,128)(2,1)} %go_hbm.1) | copy-start | bytes 98308
  3.0 0.9 %copy-start.3 = (f32[16,32,128]{2,1,0:T(8,128)S(1)}, f32[16,32,128]{2,1,0:T(8,128)}, u32[]{:S(2)}) copy-start(f32[16,32,128]{2,1,0:T(8,128)} %constant.8.clone.ct_hbm) | copy-start | bytes 786436

commit v3 on v2

--- a/solution.py
+++ b/solution.py
@@ -141,55 +141,50 @@
 
 
 class Spread:
-    NAMES = {(-1, None): 0, (-2, None): 1, (-3, None): 2, (-4, 0): 3, (-4, 1): 4, (3, None): 5, (2, None): 6, (1, None): 7}
-
     def __init__(self, slot, rows, place, to, send_sem, recv_sem):
         self.slot, self.rows, self.place, self.to = slot, rows, place, to
         self.send_sem, self.recv_sem = send_sem, recv_sem
-        self.sent = []
-
-    def copy(self, ref, name, device):
-        if name[1] is not None:
-            ref = ref.at[pl.ds(name[1] * (self.rows // 2), self.rows // 2)]
-        at = self.NAMES[name]
+        self.sent = 0
+
+    def piece(self, origin):
+        return self.slot(lax.rem(self.place + 8 + origin, 8))
+
+    def copy(self, ref, seen, device):
+        at = {-2: 0, 2: 1, -1: 2, 1: 2}.get(seen, 3)
         return pltpu.make_async_remote_copy(
-            src_ref=ref, dst_ref=ref, send_sem=self.send_sem.at[at], recv_sem=self.recv_sem.at[at],
+            src_ref=ref, dst_ref=ref, send_sem=self.send_sem, recv_sem=self.recv_sem.at[at],
             device_id=device, device_id_type=MESH,
         )
 
     def send(self, origin, distance, half=None):
-        seen = origin - distance
-        name = (-4 if seen == 4 else seen, half)
-        copy = self.copy(self.slot(lax.rem(self.place + 8 + origin, 8)), name, self.to(distance))
-        copy.start()
-        self.sent.append(copy)
-
-    def wait(self, origin, half=None):
-        self.copy(self.slot(lax.rem(self.place + 8 + origin, 8)), (origin, half), self.to(1)).wait_recv()
+        ref, rows = self.piece(origin), self.rows
+        if half is not None:
+            rows = rows // 2
+            ref = ref.at[pl.ds(half * rows, rows)]
+        self.copy(ref, origin - distance, self.to(distance)).start()
+        self.sent += rows
+
+    def wait(self, pieces, seen, total):
+        self.copy(total.at[pl.ds(0, pieces * self.rows)], seen, self.to(1)).wait_recv()
 
     def first(self):
         for distance in (2, -2, 1, -1):
             self.send(0, distance)
 
-    def middle(self):
-        self.wait(-2)
+    def middle(self, total):
+        self.wait(1, -2, total)
         self.send(-2, 2, 0)
         self.send(-2, 1)
-        self.wait(2)
+        self.wait(1, 2, total)
         self.send(2, -2, 1)
         self.send(2, -1)
-        self.wait(-1)
-        self.wait(1)
-
-    def last(self):
-        self.wait(-3)
-        self.wait(3)
-        self.wait(-4, 0)
-        self.wait(-4, 1)
-
-    def drain(self):
-        for copy in self.sent:
-            copy.wait_send()
+        self.wait(2, 1, total)
+
+    def last(self, total):
+        self.wait(3, 3, total)
+
+    def drain(self, total):
+        self.copy(total.at[pl.ds(0, self.sent)], 1, self.to(1)).wait_send()
 
 
 def kernel(
@@ -197,8 +192,8 @@
     wg_ref, fg_ref,
     go_v, taps_v, w_v, f_v, g_v, ct_v, tokb, gtb, gtx, qvb, qvx, tb, acc, bv, yb, fs, zb, gp,
     rown, rsend, rrecv, fown, fsend, frecv,
-    local_sem, ra_s, ra_r, rb_s, rb_r, ga_s, ga_r, gb_s, gb_r, qa_s, qa_r, qb_s, qb_r,
-    pair_s, pair_r, sib_s, sib_r, tr_s, tr_r, tx_s, tx_r, tx2_s, tx2_r, ts_s, ts_r,
+    local_sem, spread_s, tok_a_r, tok_b_r, gate_a_r, gate_b_r, proj_a_r, proj_b_r,
+    pair_s, pair_r, sib_s, sib_r, tr_s, tr_r, tx_s, tx_r, tx2_r, ts_s, ts_r,
 ):
     ctx, ch = lax.axis_index("ctx"), lax.axis_index("ch")
     xl, z = ctx // 8, lax.rem(ctx, 8)
@@ -283,22 +278,25 @@
 
     pl.semaphore_wait(barrier, len(peers))
 
-    tok_a = Spread(lambda q: tokb.at[xh, q, c], 128, y, along("y"), ra_s, ra_r)
-    tok_b = Spread(lambda q: tokb.at[oh, q, c], 128, y, along("y"), rb_s, rb_r)
-    gate_a = Spread(lambda q: gtb.at[q, xl], 128, z, along("z"), ga_s, ga_r)
-    gate_b = Spread(lambda q: gtb.at[q, ox], 128, z, along("z"), gb_s, gb_r)
-    proj_a = Spread(lambda q: qvb.at[q, xl], 192, z, along("z"), qa_s, qa_r)
-    proj_b = Spread(lambda q: qvb.at[q, ox], 192, z, along("z"), qb_s, qb_r)
-
-    def sib_copy(side, index, away, core):
-        ref = tokb.at[xh if side == 0 else oh, turn(y, away), core]
-        return remote(ref, ref, sib_s.at[side, index], sib_r.at[side, index], sibling)
-
+    tok_a = Spread(lambda q: tokb.at[xh, q, c], 128, y, along("y"), spread_s.at[0], tok_a_r)
+    tok_b = Spread(lambda q: tokb.at[oh, q, c], 128, y, along("y"), spread_s.at[1], tok_b_r)
+    gate_a = Spread(lambda q: gtb.at[q, xl], 128, z, along("z"), spread_s.at[2], gate_a_r)
+    gate_b = Spread(lambda q: gtb.at[q, ox], 128, z, along("z"), spread_s.at[3], gate_b_r)
+    proj_a = Spread(lambda q: qvb.at[q, xl], 192, z, along("z"), spread_s.at[4], proj_a_r)
+    proj_b = Spread(lambda q: qvb.at[q, ox], 192, z, along("z"), spread_s.at[5], proj_b_r)
+
+    total = w_v.at[0]
     index_of = {0: 0, -1: 1, -2: 2, -3: 3, -4: 4, 3: 5, 2: 6, 1: 7}
 
-    def to_sibling(side, aways):
+    def sib_copy(ref, group):
+        return remote(ref, ref, sib_s.at[0], sib_r.at[group], sibling)
+
+    def to_sibling(side, aways, group):
         for away in aways:
-            sib_copy(side, index_of[away], away, c).start()
+            sib_copy(tokb.at[xh if side == 0 else oh, turn(y, away), c], group).start()
+
+    def from_sibling(pieces, group):
+        sib_copy(total.at[pl.ds(0, 128 * pieces)], group).wait_recv()
 
     tok_pair_out = remote(tokb.at[xh, y, c], tokb.at[xh, y, c], pair_s.at[0], pair_r.at[0], h_partner)
     tok_pair_in = remote(tokb.at[oh, y, c], tokb.at[oh, y, c], pair_s.at[0], pair_r.at[0], h_partner)
@@ -310,7 +308,7 @@
     def turn_copy(away):
         q = turn(y, away)
         return remote(
-            tokb.at[xh, q, c], tb.at[xh, c, xl, z], tr_s.at[index_of[away]], tr_r.at[z], dev(xh, xl, y, q, c)
+            tokb.at[xh, q, c], tb.at[xh, c, xl, z], tr_s.at[0], tr_r.at[0], dev(xh, xl, y, q, c)
         )
 
     def turned_over(aways):
@@ -326,46 +324,48 @@
                 turn_copy(away).start()
 
     def project(aways):
-        total = None
+        summed = None
         for away in aways:
             for side in range(2):
-                sib_copy(side, index_of[away], away, oc).wait_recv()
                 q = turn(y, away)
                 h = xh if side == 0 else oh
                 left = jnp.concatenate([tokb[h, q, 0], tokb[h, q, 1]], axis=1)
                 rows = pl.ds(pl.multiple_of((h * 8 + q) * 256, 256), 256)
                 right = jnp.concatenate([w_v[j, rows, :] for j in range(3)], axis=1)
                 term = jnp.dot(left, right, preferred_element_type=F32)
-                total = term if total is None else total + term
-        return total
+                summed = term if summed is None else summed + term
+        return summed
 
     tok_pair_out.start()
     tok_a.first()
-    to_sibling(0, [0])
+    to_sibling(0, [0], 0)
     gate_out.start()
     gate_a.first()
     turned_over([0])
     tok_pair_in.wait_recv()
     tok_b.first()
-    to_sibling(1, [0])
+    to_sibling(1, [0], 0)
     gate_in.wait_recv()
     gate_b.first()
     loads[0].wait()
     near, far = [-2, 2, -1, 1], [-3, 3, -4]
-    tok_a.middle()
-    to_sibling(0, near)
+    tok_a.middle(total)
+    to_sibling(0, near, 1)
     turned_over(near)
+    from_sibling(2, 0)
     acc[...] = project([0])
-    tok_b.middle()
-    to_sibling(1, near)
-    gate_a.middle()
-    gate_b.middle()
-    tok_a.last()
-    to_sibling(0, far)
+    tok_b.middle(total)
+    to_sibling(1, near, 1)
+    gate_a.middle(total)
+    gate_b.middle(total)
+    tok_a.last(total)
+    to_sibling(0, far, 2)
     turned_over(far)
+    from_sibling(8, 1)
     acc[...] += project(near)
-    tok_b.last()
-    to_sibling(1, far)
+    tok_b.last(total)
+    to_sibling(1, far, 2)
+    from_sibling(6, 2)
     projected = (acc[...] + project(far)).astype(BF16).astype(F32)
 
     qp, kp, vp = projected[:, :128], projected[:, 128:256], projected[:, 256:]
@@ -387,37 +387,35 @@
 
     def along_x(way, k):
         ref = block_of(xh, c, xl, k)
-        return remote(ref, ref, tx_s.at[way, k], tx_r.at[way, k], x_right if way == 0 else x_left)
+        return remote(ref, ref, tx_s.at[0], tx_r.at[way, k], x_right if way == 0 else x_left)
 
     def from_x(way, k):
         ref = block_of(down_h, c, down_l, k) if way == 0 else block_of(up_h, c, up_l, k)
-        return remote(ref, ref, tx_s.at[way, k], tx_r.at[way, k], x_right if way == 0 else x_left)
+        return remote(ref, ref, tx_s.at[0], tx_r.at[way, k], x_right if way == 0 else x_left)
 
     def half_on(way, k):
         h, l = (down_h, down_l) if way == 0 else (up_h, up_l)
         ref = tb.at[h, c, l, pl.ds(PER * k + PER // 2 * way, PER // 2)]
-        return remote(ref, ref, tx2_s.at[way, k], tx2_r.at[way, k], x_right if way == 0 else x_left)
-
-    def half_from(way, k):
-        ref = tb.at[oh, c, xl, pl.ds(PER * k + PER // 2 * way, PER // 2)]
-        return remote(ref, ref, tx2_s.at[way, k], tx2_r.at[way, k], x_right if way == 0 else x_left)
+        return remote(ref, ref, tx_s.at[0], tx2_r.at[k], x_right if way == 0 else x_left)
+
+    def across(k):
+        ref = block_of(oh, c, xl, k)
+        return remote(ref, ref, tx_s.at[0], tx2_r.at[k], x_right)
 
     piece_at = [(xh, xl), (down_h, down_l), (up_h, up_l), (oh, xl)]
 
     def t_sibling(piece, k, core):
         h, l = piece_at[piece]
         ref = block_of(h, core, l, k)
-        return remote(ref, ref, ts_s.at[piece, k], ts_r.at[piece, k], sibling)
+        return remote(ref, ref, ts_s.at[0], ts_r.at[0], sibling)
+
+    def count(s, r, rows):
+        ref = total.at[pl.ds(0, rows)]
+        return remote(ref, ref, s, r, sibling)
 
     def round_x_first():
+        count(tr_s.at[0], tr_r.at[0], 7 * 128).wait_recv()
         for k in range(CHUNKS):
-            for source in range(PER * k, PER * k + PER):
-                ref = tb.at[xh, c, xl, source]
-
-                @pl.when(z != source)
-                def _():
-                    remote(ref, ref, tr_s.at[0], tr_r.at[source], sibling).wait_recv()
-
             along_x(0, k).start()
             along_x(1, k).start()
             t_sibling(0, k, c).start()
@@ -433,15 +431,14 @@
 
     def round_x_third():
         for k in range(CHUNKS):
-            half_from(0, k).wait_recv()
-            half_from(1, k).wait_recv()
+            across(k).wait_recv()
             t_sibling(3, k, c).start()
 
     round_x_first()
     proj_in.wait_recv()
     proj_b.first()
-    gate_a.last()
-    gate_b.last()
+    gate_a.last(total)
+    gate_b.last(total)
 
 
     def put_spectra(x, rows_lo, rows_hi):
@@ -482,11 +479,11 @@
 
     lax.fori_loop(0, 16, filter_tile, 0, unroll=16)
 
-    proj_a.middle()
-    proj_b.middle()
+    proj_a.middle(total)
+    proj_b.middle(total)
     round_x_second()
-    proj_a.last()
-    proj_b.last()
+    proj_a.last(total)
+    proj_b.last(total)
 
 
     def field_rows(i, carry):
@@ -505,7 +502,8 @@
         put_spectra(bottom, rows_at(64 + 16 * i), rows_at(192 + 16 * i))
         return carry
 
-    lax.fori_loop(0, 4, field_rows, 0)
+    lax.fori_loop(0, 4, field_rows, 0, unroll=4)
+    round_x_third()
     loads[2].wait()
 
     def mix_tile(k, carry):
@@ -518,25 +516,19 @@
         mixed_im = jnp.where(special, fi * si, fr * si + fi * sr)
         grad_re = jnp.where(special, tr * sr, tr * sr + ti * si)
         grad_im = jnp.where(special, ti * si, ti * sr - tr * si)
-        mixed = jnp.concatenate(
-            [
-                jnp.concatenate([mixed_re, grad_re], axis=1),
-                jnp.concatenate([mixed_im, grad_im], axis=1),
-            ],
-            axis=0,
-        ).astype(BF16)
+        mixed = jnp.concatenate([mixed_re, mixed_im], axis=0).astype(BF16)
         zb[k] = jnp.dot(g_v[k], mixed, preferred_element_type=F32)
+        yb[k] = jnp.concatenate([grad_re, grad_im], axis=0).astype(BF16)
         return carry
 
     lax.fori_loop(0, 16, mix_tile, 0, unroll=16)
-    round_x_third()
 
 
     def back_rows(i, carry):
         lo, hi = rows_at(16 * i), rows_at(128 + 16 * i)
-        spectra = [(zb[0, lo, :128], None)]
-        spectra += [(zb[k, lo, :128], zb[k, hi, :128]) for k in range(1, 16)]
-        spectra += [(zb[0, hi, :128], None)]
+        spectra = [(zb[0, lo, :], None)]
+        spectra += [(zb[k, lo, :], zb[k, hi, :]) for k in range(1, 16)]
+        spectra += [(zb[0, hi, :], None)]
         for a, restored in enumerate(real_inverse(32, spectra, half=True)):
             turned = flip(restored)
             out = rows_at(128 * a + 16 * i)
@@ -544,12 +536,10 @@
             gp[out, 128:] = (turned * qvb[a % 8, a // 8, lo, :].astype(F32)).astype(BF16)
         return carry
 
-    lax.fori_loop(0, 8, back_rows, 0)
-
-
-    for piece in range(4):
-        for k in range(CHUNKS):
-            t_sibling(piece, k, oc).wait_recv()
+    lax.fori_loop(0, 8, back_rows, 0, unroll=2)
+
+
+    count(ts_s.at[0], ts_r.at[0], 4096).wait_recv()
 
     def weight_rows(h, core):
         lhs = tb[h, core].reshape(2048, 128)
@@ -566,14 +556,15 @@
 
     def filter_grad_step(k, carry):
         sums = []
+        back = jnp.dot(g_v[k], yb[k], preferred_element_type=F32)
         for l in range(2):
             block = z + 8 * l
-            total = carry[l] + ct_v[block, pl.ds(k, 1), :] * zb[k, :128, 128:]
-            sums.append(total + ct_v[block, pl.ds(k + 16, 1), :] * zb[k, 128:, 128:])
+            total = carry[l] + ct_v[block, pl.ds(k, 1), :] * back[:128]
+            sums.append(total + ct_v[block, pl.ds(k + 16, 1), :] * back[128:])
         return tuple(sums)
 
     zero = jnp.zeros((128, 128), F32)
-    near, far = lax.fori_loop(0, 16, filter_grad_step, (zero, zero))
+    near, far = lax.fori_loop(0, 16, filter_grad_step, (zero, zero), unroll=16)
     own = jnp.where(first, near, far)
     other = jnp.where(first, far, near)
     fsend[...] = jnp.where(low64, other[:64], flip(other[64:]))
@@ -607,25 +598,11 @@
     fg_ref[...] = unfolded(fown[...], frecv[...])
 
     for spread in (tok_a, tok_b, gate_a, gate_b, proj_a, proj_b):
-        spread.drain()
+        spread.drain(total)
     for sent in (tok_pair_out, gate_out, proj_out, weight_out, filter_out):
         sent.wait_send()
-    for side in range(2):
-        for away, index in index_of.items():
-            sib_copy(side, index, away, c).wait_send()
-
-    for away in index_of:
-
-        @pl.when(turn(y, away) != z)
-        def _():
-            turn_copy(away).wait_send()
-
-    for k in range(CHUNKS):
-        for way in range(2):
-            along_x(way, k).wait_send()
-            half_on(way, k).wait_send()
-        for piece in range(4):
-            t_sibling(piece, k, c).wait_send()
+    for s, rows in ((sib_s, 16 * 128), (tr_s, 7 * 128), (tx_s, 3072), (ts_s, 4096)):
+        count(s.at[0], sib_r.at[0], rows).wait_send()
 
 
 def on_device(tables, tokens, in_weight, filter_taps, grad_out):
@@ -633,7 +610,6 @@
     vmem = pl.BlockSpec(memory_space=pltpu.VMEM)
     anywhere = pl.BlockSpec(memory_space=pltpu.HBM)
     dma = pltpu.SemaphoreType.DMA
-    ring_sems = [dma((8,)) for _ in range(12)]
     weight_grad, filter_grad = pl.pallas_call(
         kernel,
         out_shape=(
@@ -659,7 +635,7 @@
             pltpu.VMEM((16, 128, 128), BF16),
             pltpu.VMEM((16, 256, 128), BF16),
             pltpu.VMEM((16, 256, 128), F32),
-            pltpu.VMEM((16, 256, 256), F32),
+            pltpu.VMEM((16, 256, 128), F32),
             pltpu.VMEM((2048, 256), BF16),
             pltpu.VMEM((256, 256), F32),
             pltpu.VMEM((384, 128), BF16),
@@ -668,16 +644,16 @@
             pltpu.VMEM((64, 128), F32),
             pltpu.VMEM((64, 128), F32),
             dma((7,)),
-            *ring_sems,
+            dma((6,)),
+            *[dma((4,)) for _ in range(6)],
             dma((5,)), dma((5,)),
-            dma((2, 8)), dma((2, 8)),
-            dma((8,)), dma((8,)),
-            dma((2, CHUNKS)), dma((2, CHUNKS)),
-            dma((2, CHUNKS)), dma((2, CHUNKS)),
-            dma((4, CHUNKS)), dma((4, CHUNKS)),
+            dma((1,)), dma((3,)),
+            dma((1,)), dma((1,)),
+            dma((1,)), dma((2, CHUNKS)), dma((CHUNKS,)),
+            dma((1,)), dma((1,)),
         ],
         compiler_params=pltpu.CompilerParams(
-            collective_id=0, has_side_effects=True, vmem_limit_bytes=52 * 1024 * 1024
+            collective_id=0, has_side_effects=True, vmem_limit_bytes=63 * 1024 * 1024
         ),
         cost_estimate=pl.CostEstimate(flops=3_000_000_000, bytes_accessed=10_000_000, transcendentals=0),
     )(

time: 57.9 us -> 53.9 us (0.931)
  the two profiles are of different devices: /device:TPU:1 before, /device:TPU:32 now
where the time goes in v3:
time: 53.9 us; the launch traced here: 53.7 us
  Pallas kernels  49.8 us (92%)
  local copies, waits for them, and re-layouts  3.24 us (6%)
  between operations  0.64 us (1%)
    pallas_call x1, Pallas kernels, on_device(): pl.pallas_call(kernel, out_shape=(jax.ShapeDtypeStruct((3, 256, 128), F32...  49.8 us
    unnamed x2, local copies, waits for them, and re-layouts  3.24 us

profile of v3, /device:TPU:32, one launch (start us, length us, event | category | flops | bytes accessed | tf_op | source)
XLA Modules:
  0.0 53.7 jit_solution(11250636502171329558)
XLA Ops:
  0.6 49.8 %shard_map.86 = (f32[3,256,128]{2,1,0:T(8,128)}, f32[128,128]{1,0:T(8,128)}) custom-call(bf16[128,128]{1,0:T(8,128)(2,1)} %tok_hbm.1, bf16[128,128]{1,0:T(8,128)(2,1)} %go_hbm.1, f32[128,128]{1,0:T(8,128)} %taps_hbm.1, bf16[3,4096,128]{2,1,0:T(8,128)(2,1)} %bitcast.3, bf16[16,256,256]{2,1,0:T(8,128)(2,1)} %constant.6.clone.f_hbm, ...), custom_call_target="tpu_custom_call" | custom-call | flops 3000000000 | bytes 10000000 | tf_op jit(solution)/shard_map/pallas_call | solution.py:613
  50.4 1.8 %copy.11 = f32[256,3,128]{2,0,1:T(8,128)} copy(f32[256,3,128]{2,0,1:T(8,128)} %bitcast.2) | data formatting | bytes 786432
  52.2 1.5 %copy.12 = f32[128,128]{1,0:T(8,128)} copy(f32[128,128]{1,0:T(8,128)} %get-tuple-element.9) | data formatting | bytes 131072

commit v4 on v3

--- a/solution.py
+++ b/solution.py
@@ -224,6 +224,13 @@
     x_right = dev(x_up // 2, lax.rem(x_up, 2), y, z, c)
     x_left = dev(x_down // 2, lax.rem(x_down, 2), y, z, c)
 
+    own_loads = [
+        pltpu.make_async_copy(go_hbm, go_v, local_sem.at[4]),
+        pltpu.make_async_copy(taps_hbm, taps_v, local_sem.at[5]),
+        pltpu.make_async_copy(tok_hbm, tokb.at[xh, y, c], local_sem.at[6]),
+    ]
+    for load in own_loads:
+        load.start()
     barrier = pltpu.get_barrier_semaphore()
     peers = [sibling] + [along("y")(by) for by in (-2, -1, 1, 2)]
     peers += [along("z")(by) for by in range(1, 8)]
@@ -233,13 +240,6 @@
     for peer in peers:
         pl.semaphore_signal(barrier, inc=1, device_id=peer, device_id_type=MESH)
 
-    own_loads = [
-        pltpu.make_async_copy(go_hbm, go_v, local_sem.at[4]),
-        pltpu.make_async_copy(taps_hbm, taps_v, local_sem.at[5]),
-        pltpu.make_async_copy(tok_hbm, tokb.at[xh, y, c], local_sem.at[6]),
-    ]
-    for load in own_loads:
-        load.start()
     loads = [
         pltpu.make_async_copy(w_hbm, w_v, local_sem.at[0]),
         pltpu.make_async_copy(f_hbm, f_v, local_sem.at[1]),
@@ -356,11 +356,11 @@
     acc[...] = project([0])
     tok_b.middle(total)
     to_sibling(1, near, 1)
-    gate_a.middle(total)
-    gate_b.middle(total)
     tok_a.last(total)
     to_sibling(0, far, 2)
     turned_over(far)
+    gate_a.middle(total)
+    gate_b.middle(total)
     from_sibling(8, 1)
     acc[...] += project(near)
     tok_b.last(total)
@@ -653,17 +653,16 @@
             dma((1,)), dma((1,)),
         ],
         compiler_params=pltpu.CompilerParams(
-            collective_id=0, has_side_effects=True, vmem_limit_bytes=63 * 1024 * 1024
+            collective_id=0, has_side_effects=True, vmem_limit_bytes=52 * 1024 * 1024
         ),
         cost_estimate=pl.CostEstimate(flops=3_000_000_000, bytes_accessed=10_000_000, transcendentals=0),
     )(
-        tokens,
-        grad_out,
-        filter_taps,
-        jnp.transpose(in_weight, (1, 0, 2)),
-        forward,
-        inverse,
-        single,
+        *[
+            pltpu.with_memory_space_constraint(operand, pltpu.HBM)
+            for operand in (
+                tokens, grad_out, filter_taps, jnp.transpose(in_weight, (1, 0, 2)), forward, inverse, single
+            )
+        ]
     )
     return jnp.transpose(weight_grad, (1, 0, 2)), filter_grad
 

time: 53.9 us -> 50.9 us (0.944)
  the two profiles are of different devices: /device:TPU:32 before, /device:TPU:1 now
where the time goes in v4:
time: 50.9 us; the launch traced here: 50.8 us
  Pallas kernels  48.8 us (96%)
  local copies, waits for them, and re-layouts  1.38 us (3%)
  between operations  0.64 us (1%)
    pallas_call x1, Pallas kernels, on_device(): pl.pallas_call(kernel, out_shape=(jax.ShapeDtypeStruct((3, 256, 128), F32...  48.8 us
    unnamed x2, local copies, waits for them, and re-layouts  1.38 us

profile of v4, /device:TPU:1, one launch (start us, length us, event | category | flops | bytes accessed | tf_op | source)
XLA Modules:
  0.0 50.8 jit_solution(14417046397262656592)
XLA Ops:
  0.6 48.8 %shard_map.86 = (f32[3,256,128]{2,1,0:T(8,128)S(1)}, f32[128,128]{1,0:T(8,128)S(1)}) custom-call(bf16[128,128]{1,0:T(8,128)(2,1)} %tok_hbm.1, bf16[128,128]{1,0:T(8,128)(2,1)} %go_hbm.1, f32[128,128]{1,0:T(8,128)} %taps_hbm.1, bf16[3,4096,128]{2,1,0:T(8,128)(2,1)} %bitcast.3, bf16[16,256,256]{2,1,0:T(8,128)(2,1)} %constant.6.clone.f_hbm, ...), custom_call_target="tpu_custom_call" | custom-call | flops 3000000000 | bytes 10000000 | tf_op jit(solution)/shard_map/pallas_call | solution.py:613
  49.4 0.7 %copy.11 = f32[256,3,128]{2,0,1:T(8,128)} copy(f32[256,3,128]{2,0,1:T(8,128)S(1)} %bitcast.2) | data formatting | bytes 786432
  50.2 0.6 %copy.12 = f32[128,128]{1,0:T(8,128)} copy(f32[128,128]{1,0:T(8,128)S(1)} %get-tuple-element.9) | data formatting | bytes 131072

commit v5 on v4

--- a/solution.py
+++ b/solution.py
@@ -227,7 +227,7 @@
     own_loads = [
         pltpu.make_async_copy(go_hbm, go_v, local_sem.at[4]),
         pltpu.make_async_copy(taps_hbm, taps_v, local_sem.at[5]),
-        pltpu.make_async_copy(tok_hbm, tokb.at[xh, y, c], local_sem.at[6]),
+        pltpu.make_async_copy(tok_hbm, tokb.at[c, y, xh], local_sem.at[6]),
     ]
     for load in own_loads:
         load.start()
@@ -278,8 +278,8 @@
 
     pl.semaphore_wait(barrier, len(peers))
 
-    tok_a = Spread(lambda q: tokb.at[xh, q, c], 128, y, along("y"), spread_s.at[0], tok_a_r)
-    tok_b = Spread(lambda q: tokb.at[oh, q, c], 128, y, along("y"), spread_s.at[1], tok_b_r)
+    tok_a = Spread(lambda q: tokb.at[c, q, xh], 128, y, along("y"), spread_s.at[0], tok_a_r)
+    tok_b = Spread(lambda q: tokb.at[c, q, oh], 128, y, along("y"), spread_s.at[1], tok_b_r)
     gate_a = Spread(lambda q: gtb.at[q, xl], 128, z, along("z"), spread_s.at[2], gate_a_r)
     gate_b = Spread(lambda q: gtb.at[q, ox], 128, z, along("z"), spread_s.at[3], gate_b_r)
     proj_a = Spread(lambda q: qvb.at[q, xl], 192, z, along("z"), spread_s.at[4], proj_a_r)
@@ -291,15 +291,15 @@
     def sib_copy(ref, group):
         return remote(ref, ref, sib_s.at[0], sib_r.at[group], sibling)
 
-    def to_sibling(side, aways, group):
+    def to_sibling(aways, group):
         for away in aways:
-            sib_copy(tokb.at[xh if side == 0 else oh, turn(y, away), c], group).start()
+            sib_copy(tokb.at[c, turn(y, away)], group).start()
 
     def from_sibling(pieces, group):
         sib_copy(total.at[pl.ds(0, 128 * pieces)], group).wait_recv()
 
-    tok_pair_out = remote(tokb.at[xh, y, c], tokb.at[xh, y, c], pair_s.at[0], pair_r.at[0], h_partner)
-    tok_pair_in = remote(tokb.at[oh, y, c], tokb.at[oh, y, c], pair_s.at[0], pair_r.at[0], h_partner)
+    tok_pair_out = remote(tokb.at[c, y, xh], tokb.at[c, y, xh], pair_s.at[0], pair_r.at[0], h_partner)
+    tok_pair_in = remote(tokb.at[c, y, oh], tokb.at[c, y, oh], pair_s.at[0], pair_r.at[0], h_partner)
     gate_out = remote(gtx, gtb.at[z, xl], pair_s.at[1], pair_r.at[1], l_partner)
     gate_in = remote(gtx, gtb.at[z, ox], pair_s.at[1], pair_r.at[1], l_partner)
     proj_out = remote(qvx, qvb.at[z, xl], pair_s.at[2], pair_r.at[2], l_partner)
@@ -308,7 +308,7 @@
     def turn_copy(away):
         q = turn(y, away)
         return remote(
-            tokb.at[xh, q, c], tb.at[xh, c, xl, z], tr_s.at[0], tr_r.at[0], dev(xh, xl, y, q, c)
+            tokb.at[c, q, xh], tb.at[xh, c, xl, z], tr_s.at[0], tr_r.at[0], dev(xh, xl, y, q, c)
         )
 
     def turned_over(aways):
@@ -317,7 +317,7 @@
 
             @pl.when(q == z)
             def _():
-                tb[xh, c, xl, z] = tokb[xh, q, c]
+                tb[xh, c, xl, z] = tokb[c, q, xh]
 
             @pl.when(q != z)
             def _():
@@ -329,7 +329,7 @@
             for side in range(2):
                 q = turn(y, away)
                 h = xh if side == 0 else oh
-                left = jnp.concatenate([tokb[h, q, 0], tokb[h, q, 1]], axis=1)
+                left = jnp.concatenate([tokb[0, q, h], tokb[1, q, h]], axis=1)
                 rows = pl.ds(pl.multiple_of((h * 8 + q) * 256, 256), 256)
                 right = jnp.concatenate([w_v[j, rows, :] for j in range(3)], axis=1)
                 term = jnp.dot(left, right, preferred_element_type=F32)
@@ -338,33 +338,30 @@
 
     tok_pair_out.start()
     tok_a.first()
-    to_sibling(0, [0], 0)
     gate_out.start()
     gate_a.first()
     turned_over([0])
     tok_pair_in.wait_recv()
     tok_b.first()
-    to_sibling(1, [0], 0)
+    to_sibling([0], 0)
     gate_in.wait_recv()
     gate_b.first()
     loads[0].wait()
     near, far = [-2, 2, -1, 1], [-3, 3, -4]
     tok_a.middle(total)
-    to_sibling(0, near, 1)
     turned_over(near)
     from_sibling(2, 0)
     acc[...] = project([0])
     tok_b.middle(total)
-    to_sibling(1, near, 1)
+    to_sibling(near, 1)
     tok_a.last(total)
-    to_sibling(0, far, 2)
     turned_over(far)
     gate_a.middle(total)
     gate_b.middle(total)
     from_sibling(8, 1)
     acc[...] += project(near)
     tok_b.last(total)
-    to_sibling(1, far, 2)
+    to_sibling(far, 2)
     from_sibling(6, 2)
     projected = (acc[...] + project(far)).astype(BF16).astype(F32)
 
@@ -434,9 +431,9 @@
             across(k).wait_recv()
             t_sibling(3, k, c).start()
 
-    round_x_first()
     proj_in.wait_recv()
     proj_b.first()
+    round_x_first()
     gate_a.last(total)
     gate_b.last(total)
 

time: 50.9 us -> 50.9 us (level)
  no operation moved by 1% of the time
where the time goes in v5:
time: 50.9 us; the launch traced here: 50.6 us
  Pallas kernels  48.5 us (95%)
  local copies, waits for them, and re-layouts  1.38 us (3%)
  between operations  0.64 us (1%)
    pallas_call x1, Pallas kernels, on_device(): pl.pallas_call(kernel, out_shape=(jax.ShapeDtypeStruct((3, 256, 128), F32...  48.5 us
    unnamed x2, local copies, waits for them, and re-layouts  1.38 us

profile of v5, /device:TPU:1, one launch (start us, length us, event | category | flops | bytes accessed | tf_op | source)
XLA Modules:
  0.0 50.6 jit_solution(961882157443012409)
XLA Ops:
  0.6 48.5 %shard_map.86 = (f32[3,256,128]{2,1,0:T(8,128)S(1)}, f32[128,128]{1,0:T(8,128)S(1)}) custom-call(bf16[128,128]{1,0:T(8,128)(2,1)} %tok_hbm.1, bf16[128,128]{1,0:T(8,128)(2,1)} %go_hbm.1, f32[128,128]{1,0:T(8,128)} %taps_hbm.1, bf16[3,4096,128]{2,1,0:T(8,128)(2,1)} %bitcast.3, bf16[16,256,256]{2,1,0:T(8,128)(2,1)} %constant.6.clone.f_hbm, ...), custom_call_target="tpu_custom_call" | custom-call | flops 3000000000 | bytes 10000000 | tf_op jit(solution)/shard_map/pallas_call | solution.py:610
  49.2 0.7 %copy.11 = f32[256,3,128]{2,0,1:T(8,128)} copy(f32[256,3,128]{2,0,1:T(8,128)S(1)} %bitcast.2) | data formatting | bytes 786432
  49.9 0.6 %copy.12 = f32[128,128]{1,0:T(8,128)} copy(f32[128,128]{1,0:T(8,128)S(1)} %get-tuple-element.9) | data formatting | bytes 131072
